TPU v7x, 32 devices: a whole 2x2x4 slice. The times are simulated.
32 devices in a mesh: rep: 2 (over y), node: 4 (over x, core), local: 4 (over z).
Axes of the slice: x: 2, y: 2, z: 4, core: 2. Of those that a mesh axis runs over, the one named last changes fastest.
Arguments:
- tokens: bfloat16 [8192, 4096], P(('rep', 'node', 'local')), parts along dimension 0, may hold values from -6 to 6
- routes: int32 [8192, 4], P(('rep', 'node', 'local')), parts along dimension 0, may hold values from 0 to 15, all different within a row; in each aligned block of 256 rows (0 to 255, 256 to 511, ...) at most 128 rows name the same one
- gates: int32 [8192, 4], P(('rep', 'node', 'local')), parts along dimension 0, may hold values from 4096 to 32767
- w_down: bfloat16 [4096, 1024], P('local'), may hold values from -0.09375 to 0.09375
- w_up: bfloat16 [1024, 4096], P(None, 'local'), may hold values from -0.1875 to 0.1875
- expert_gate: bfloat16 [16, 1024, 768], P(('node', 'local')), may hold values from -0.1875 to 0.1875
- expert_up: bfloat16 [16, 1024, 768], P(('node', 'local')), may hold values from -0.1875 to 0.1875
- expert_down: bfloat16 [16, 768, 1024], P(('node', 'local')), may hold values from -0.21875 to 0.21875
Outputs:
- mixed: bfloat16 [8192, 4096], P(('rep', 'node', 'local')), parts along dimension 0
There are 2 independent parts, one for each index of `rep`. A program takes and returns all parts, laid end to end along the dimension named above; an argument that names none is the same for every part. Nothing has to cross between parts.
Inputs may be any that keep to these rules, and one draw needn't show every extreme that they name: Within the 256 rows of one device no expert is named by more than 128 routes, and in every draw some device sends exactly 128 routes to some expert; the routes of one token are distinct.
All inputs are finite; a program needn't handle non-finite values.
Results may differ from a plain program's by a relative error of at most 0.0068.
Values may be sent and summed in bfloat16 or wider, within the bound.
A program may use at most 128 MiB of HBM per device.

v0:
```python
import jax
import jax.numpy as jnp
from jax import lax
from jax.sharding import PartitionSpec as P


def local(tokens, routes, gates, w_down, w_up, expert_gate, expert_up, expert_down):
    tok_rows = tokens.shape[0]
    top_k = routes.shape[1]
    owners = lax.axis_size("node") * lax.axis_size("local")
    exp_local = expert_gate.shape[0]
    experts_all = owners * exp_local
    latent_width = w_down.shape[1]
    capacity = 2 * tok_rows * top_k // experts_all
    tok32 = tokens.astype(jnp.float32)
    normed = (tok32 * lax.rsqrt(jnp.mean(tok32 * tok32, axis=-1, keepdims=True) + 1e-06)).astype(
        jnp.bfloat16
    )
    latent = jnp.dot(
        normed,
        lax.all_gather(w_down, "local", axis=0, tiled=True),
        preferred_element_type=jnp.float32,
    ).astype(jnp.bfloat16)
    flat_routes = routes.reshape(-1)
    onehot = (flat_routes[:, None] == jnp.arange(experts_all, dtype=jnp.int32)[None, :]).astype(
        jnp.int32
    )
    ranks = jnp.cumsum(onehot, axis=0) - 1
    slot = jnp.sum(ranks * onehot, axis=1)
    target = flat_routes * capacity + slot
    source_rows = jnp.repeat(latent, top_k, axis=0)
    outgoing = (
        jnp.zeros((experts_all * capacity, latent_width), jnp.bfloat16).at[target].set(source_rows)
    )
    outgoing = outgoing.reshape(owners, exp_local, capacity, latent_width)
    arrived = lax.all_to_all(outgoing, ("node", "local"), split_axis=0, concat_axis=0, tiled=True)
    gate = jnp.einsum("sjml,jlf->sjmf", arrived, expert_gate, preferred_element_type=jnp.float32)
    upper = jnp.einsum("sjml,jlf->sjmf", arrived, expert_up, preferred_element_type=jnp.float32)
    hidden = (jax.nn.silu(gate) * upper).astype(jnp.bfloat16)
    answer = jnp.einsum("sjmf,jfl->sjml", hidden, expert_down, preferred_element_type=jnp.float32)
    back = lax.all_to_all(
        answer.astype(jnp.bfloat16), ("node", "local"), split_axis=0, concat_axis=0, tiled=True
    )
    back_rows = back.reshape(experts_all * capacity, latent_width)
    picked = back_rows[target].reshape(tok_rows, top_k, latent_width).astype(jnp.float32)
    scale = gates.astype(jnp.float32) * (1.0 / 32768.0)
    combined = jnp.sum(picked * scale[:, :, None], axis=1).astype(jnp.bfloat16)
    return (
        tok32
        + jnp.dot(
            combined,
            lax.all_gather(w_up, "local", axis=1, tiled=True),
            preferred_element_type=jnp.float32,
        )
    ).astype(jnp.bfloat16)


def solution(mesh):
    return jax.shard_map(
        local,
        mesh=mesh,
        in_specs=(
            P(("rep", "node", "local"), None),
            P(("rep", "node", "local"), None),
            P(("rep", "node", "local"), None),
            P("local", None),
            P(None, "local"),
            P(("node", "local"), None, None),
            P(("node", "local"), None, None),
            P(("node", "local"), None, None),
        ),
        out_specs=P(("rep", "node", "local"), None),
        check_vma=False,
    )
```

profile of v0, /device:TPU:0, one launch (start us, length us, event | category | flops | bytes accessed | tf_op | source)
XLA Modules:
  0.0 546.0 jit_solution(3549634197997157961)
XLA Ops:
  6.5 0.0 copy-start
  6.5 0.0 all-gather.3.cloned.1.call-start
  6.5 0.7 all-gather.3.cloned.1.call-update
  7.3 0.8 copy.19
  8.1 0.1 eq.29
  8.2 0.1 eq.25
  8.3 4.5 reduce-window.6
  12.9 0.1 slice.10
  12.9 0.1 copy.21
  13.1 0.1 copy.22
  13.2 0.7 broadcast_multiply_fusion
  13.9 0.1 copy.18
  14.0 0.1 mul.53
  14.1 0.1 add_add_fusion
  14.3 2.1 fusion.5
  16.4 144.9 %all-gather.3.cloned.1.call-done = bf16[4096,1024]{1,0:T(8,128)(2,1)} async-done(((bf16[1024,1024]{1,0:T(8,128)(2,1)}), bf16[4096,1024]{1,0:T(8,128)(2,1)}) %all-gather.3.cloned.1.call-update) | async-done | bytes 8388624 | tf_op jit(solution)/shard_map/all_gather | solution.py:21
  161.3 6.4 %fusion.29 = bf16[256,1024]{1,0:T(8,128)(2,1)S(1)} fusion(bf16[4096,1024]{1,0:T(8,128)(2,1)} %all-gather.3.cloned.1.call-done, bf16[256,4096]{1,0:T(8,128)(2,1)} %param.8, f32[256]{0:T(256)S(1)} %add_rsqrt_fusion), kind=kOutput, calls=%fused_computation.30 | convolution fusion | flops 2150891520 | bytes 11011072 | tf_op jit(solution)/shard_map/dot_general | solution.py:19
  167.7 2.0 broadcast_in_dim.5
  169.7 4.0 reshape.111
  173.6 8.6 %scatter_custom_fusion = bf16[2048,1024]{1,0:T(8,128)(2,1)} fusion(s32[1024]{0:T(1024)S(1)} %bitcast.95, bf16[1024,1024]{1,0:T(8,128)(2,1)} %reshape.111, bf16[]{:T(256)} %constant.10.clone.1), kind=kCustom, calls=%fused_computation.25 | custom fusion | bytes 4194816 | tf_op jit(solution)/shard_map/scatter | solution.py:33
  182.2 0.0 copy-start.2
  182.2 4.7 all-to-all-start
  186.9 0.2 all-gather.5.cloned.1.call-start
  187.1 0.5 all-gather.5.cloned.1.call-update
  187.7 204.4 %all-to-all-done = bf16[16,1,128,1024]{3,2,1,0:T(8,128)(2,1)} async-done(((bf16[16,1,128,1024]{3,2,1,0:T(8,128)(2,1)}), bf16[16,1,128,1024]{3,2,1,0:T(8,128)(2,1)}, u32[]{:S(2)}, u32[]{:S(2)}) %all-to-all-start) | async-done | bytes 4194336 | tf_op jit(solution)/shard_map/all_to_all | solution.py:36
  392.1 0.0 copy-done.2
  392.1 8.4 %fusion.7 = f32[16,128,768]{2,1,0:T(8,128)} fusion(bf16[16,1,128,1024]{3,2,1,0:T(8,128)(2,1)} %all-to-all-done, bf16[1,1024,768]{2,1,0:T(8,128)(2,1)S(1)} %copy-done.2), kind=kOutput, calls=%fused_computation.15 | convolution fusion | flops 3221225472 | bytes 12058624 | tf_op jit(solution)/shard_map/sjml,jlf->sjmf/dot_general | solution.py:38
  400.5 0.0 copy-done
  400.5 13.1 %convert_bitcast_fusion = bf16[16,1,128,1024]{3,2,1,0:T(8,128)(2,1)} fusion(f32[16,128,768]{2,1,0:T(8,128)} %fusion.7, bf16[16,1,128,1024]{3,2,1,0:T(8,128)(2,1)} %all-to-all-done, bf16[1,768,1024]{2,1,0:T(8,128)(2,1)S(1)} %copy-done, bf16[1,1024,768]{2,1,0:T(8,128)(2,1)} %param.13), kind=kOutput, calls=%fused_computation.20 | convolution fusion | flops 6453985280 | bytes 17825792 | tf_op jit(solution)/shard_map/sjmf,jfl->sjml/dot_general | solution.py:40
  413.6 0.0 copy-start.1
  413.6 5.0 all-to-all-start.1
  418.6 0.0 copy-done.1
  418.6 0.1 copy.24
  418.8 94.2 %all-to-all-done.1 = bf16[16,1,128,1024]{3,2,1,0:T(8,128)(2,1)} async-done(((bf16[16,1,128,1024]{3,2,1,0:T(8,128)(2,1)}), bf16[16,1,128,1024]{3,2,1,0:T(8,128)(2,1)}, u32[]{:S(2)}, u32[]{:S(2)}) %all-to-all-start.1) | async-done | bytes 4194336 | tf_op jit(solution)/shard_map/all_to_all | solution.py:41
  513.0 8.7 %gather_fusion = bf16[1024,1024]{1,0:T(8,128)(2,1)} fusion(bf16[2048,1024]{1,0:T(8,128)(2,1)} %bitcast.25, s32[1024]{0:T(1024)S(1)} %broadcast_clamp_fusion), kind=kCustom, calls=%fused_computation | custom fusion | bytes 4198400 | tf_op jit(solution)/shard_map/gather | solution.py:45
  521.7 4.8 reshape.98
  526.5 4.9 multiply_reduce_fusion
  531.5 0.0 all-gather.5.cloned.1.call-done
  531.5 7.6 %fusion.4 = bf16[256,4096]{1,0:T(8,128)(2,1)} fusion(bf16[1024,4096]{1,0:T(8,128)(2,1)} %all-gather.5.cloned.1.call-done, bf16[256,4096]{1,0:T(8,128)(2,1)} %param.8, bf16[256,1024]{1,0:T(8,128)(2,1)S(1)} %multiply_reduce_fusion), kind=kOutput, calls=%fused_computation.12 | convolution fusion | flops 2150629376 | bytes 13107200 | tf_op jit(solution)/shard_map/dot_general | solution.py:50
  (8 shorter events, 0.1 us)
Async XLA Ops:
  6.5 393.9 %copy-start = (bf16[1,768,1024]{2,1,0:T(8,128)(2,1)S(1)}, bf16[1,768,1024]{2,1,0:T(8,128)(2,1)}, u32[]{:S(2)}) copy-start(bf16[1,768,1024]{2,1,0:T(8,128)(2,1)} %param.15) | copy-start | bytes 4718596
  6.5 154.8 %all-gather.3.cloned.1.call-start = ((), (), s32[]{:S(2)}) async-start(), calls=%async_computation.2 | async-start | bytes 10485760 | tf_op jit(solution)/shard_map/all_gather | solution.py:21
  182.2 209.9 %copy-start.2 = (bf16[1,1024,768]{2,1,0:T(8,128)(2,1)S(1)}, bf16[1,1024,768]{2,1,0:T(8,128)(2,1)}, u32[]{:S(2)}) copy-start(bf16[1,1024,768]{2,1,0:T(8,128)(2,1)} %param.14) | copy-start | bytes 4718596
  182.2 209.9 %all-to-all-start = ((bf16[16,1,128,1024]{3,2,1,0:T(8,128)(2,1)}), bf16[16,1,128,1024]{3,2,1,0:T(8,128)(2,1)}, u32[]{:S(2)}, u32[]{:S(2)}) async-start(bf16[16,1,128,1024]{3,2,1,0:T(8,128)(2,1)} %bitcast.91), calls=%async_computation | async-start | bytes 8388608 | tf_op jit(solution)/shard_map/all_to_all | solution.py:36
  186.9 344.6 %all-gather.5.cloned.1.call-start = ((), (), s32[]{:S(2)}) async-start(), calls=%async_computation.3 | async-start | bytes 10485760 | tf_op jit(solution)/shard_map/all_gather | solution.py:52
  413.6 5.0 copy-start.1
  413.6 99.4 %all-to-all-start.1 = ((bf16[16,1,128,1024]{3,2,1,0:T(8,128)(2,1)}), bf16[16,1,128,1024]{3,2,1,0:T(8,128)(2,1)}, u32[]{:S(2)}, u32[]{:S(2)}) async-start(bf16[16,1,128,1024]{3,2,1,0:T(8,128)(2,1)} %convert_bitcast_fusion), calls=%async_computation.1 | async-start | bytes 8388608 | tf_op jit(solution)/shard_map/all_to_all | solution.py:41
Sparse Core Ops, SparseCore 0:
  8.9 152.3 all-gather.2
  189.3 226.4 all-gather.4
where the time goes:
time: 547 us; the launch traced here: 546 us
  waiting for transfers between devices  445 us (81%)
  matrix products  35.5 us (6%)
  local copies, waits for them, and re-layouts  29.8 us (5%)
  between operations  13.5 us (2%)
  other arithmetic  12.4 us (2%)
  starting transfers between devices  9.87 us (2%)
    all_to_all x1, waiting for transfers between devices, local(): lax.all_to_all(outgoing, ('node', 'local'), split_axis=0, concat_axis=0,...  204 us
    all_gather x1, waiting for transfers between devices, local(): lax.all_gather(w_down, 'local', axis=0, tiled=True)  145 us
    all_to_all x1, waiting for transfers between devices, local(): lax.all_to_all(answer.astype(jnp.bfloat16), ('node', 'local'), split_axis...  94.2 us
    dot_general x1, matrix products, local(): jnp.einsum('sjmf,jfl->sjml', hidden, expert_down, preferred_element_type=...  13.1 us
  transfers between devices with their start and end apart: 4, of which 3 were waited for; matrix products, arithmetic and copies ran while one was open for 9% of the time, Pallas kernels for 0%

commit v1 on v0

v1 whole, which is shorter than its diff:
```python
import jax
import jax.numpy as jnp
from jax import lax
from jax.sharding import PartitionSpec as P

GROUP = ("node", "local")


def gather_weight(w, axis):
    copies = lax.axis_size("rep") * lax.axis_size("node")
    part = w.shape[0] // copies
    mine = lax.axis_index("rep") * lax.axis_size("node") + lax.axis_index("node")
    piece = lax.dynamic_slice_in_dim(w, mine * part, part, axis=0)
    whole = lax.all_gather(piece, ("local", "rep", "node"), axis=0, tiled=True)
    if axis == 0:
        return whole
    n_local = lax.axis_size("local")
    return whole.reshape(n_local, w.shape[0], w.shape[1])


def local(tokens, routes, gates, w_down, w_up, expert_gate, expert_up, expert_down):
    tok_rows = tokens.shape[0]
    top_k = routes.shape[1]
    owners = lax.axis_size("node") * lax.axis_size("local")
    exp_local = expert_gate.shape[0]
    experts_all = owners * exp_local
    width = w_down.shape[1]
    capacity = 2 * tok_rows * top_k // experts_all
    me = lax.axis_index("node") * lax.axis_size("local") + lax.axis_index("local")

    coded = jnp.concatenate([routes.T, gates.T], axis=0)
    coded = lax.all_gather(coded, GROUP, axis=0)
    all_routes, all_gates = coded[:, :top_k], coded[:, top_k:]

    tok32 = tokens.astype(jnp.float32)
    normed = (tok32 * lax.rsqrt(jnp.mean(tok32 * tok32, axis=-1, keepdims=True) + 1e-06)).astype(
        jnp.bfloat16
    )
    down = gather_weight(w_down, 0)
    latent = jnp.dot(normed, down, preferred_element_type=jnp.float32).astype(jnp.bfloat16)
    everyone = lax.all_gather(latent, GROUP, axis=0)

    total = None
    for j in range(exp_local):
        named = all_routes == me * exp_local + j
        mask = jnp.any(named, axis=1)
        weight = jnp.sum(jnp.where(named, all_gates, 0), axis=1).astype(jnp.float32) * (
            1.0 / 32768.0
        )
        rank = jnp.where(mask, jnp.cumsum(mask.astype(jnp.int32), axis=1) - 1, -1)
        pick = rank[:, None, :] == jnp.arange(capacity, dtype=jnp.int32)[None, :, None]
        pick16 = pick.astype(jnp.bfloat16)
        row_weight = jnp.sum(jnp.where(pick, weight[:, None, :], 0.0), axis=2)
        rows = jnp.einsum(
            "sct,stl->scl", pick16, everyone, preferred_element_type=jnp.float32
        ).astype(jnp.bfloat16)
        rows = rows.reshape(owners * capacity, width)
        gate = jnp.dot(rows, expert_gate[j], preferred_element_type=jnp.float32)
        upper = jnp.dot(rows, expert_up[j], preferred_element_type=jnp.float32)
        hidden = (jax.nn.silu(gate) * upper).astype(jnp.bfloat16)
        answer = jnp.dot(hidden, expert_down[j], preferred_element_type=jnp.float32)
        answer = (answer * row_weight.reshape(-1, 1)).astype(jnp.bfloat16)
        placed = jnp.einsum(
            "sct,scl->stl",
            pick16,
            answer.reshape(owners, capacity, width),
            preferred_element_type=jnp.float32,
        )
        total = placed if total is None else total + placed
    total = total.astype(jnp.bfloat16).reshape(owners * tok_rows, width)
    combined = lax.psum_scatter(total, GROUP, scatter_dimension=0, tiled=True)

    up = gather_weight(w_up, 1)
    product = jnp.einsum("tl,clw->tcw", combined, up, preferred_element_type=jnp.float32)
    return (tok32 + product.reshape(tok_rows, -1)).astype(jnp.bfloat16)


def solution(mesh):
    return jax.shard_map(
        local,
        mesh=mesh,
        in_specs=(
            P(("rep", "node", "local"), None),
            P(("rep", "node", "local"), None),
            P(("rep", "node", "local"), None),
            P("local", None),
            P(None, "local"),
            P(("node", "local"), None, None),
            P(("node", "local"), None, None),
            P(("node", "local"), None, None),
        ),
        out_specs=P(("rep", "node", "local"), None),
        check_vma=False,
    )
```

time: 547 us -> 374 us (0.68)
  waiting for transfers between devices: 445 us -> 260 us
  blocking collectives: 0 us -> 33.7 us
  local copies, waits for them, and re-layouts: 29.8 us -> 15.8 us
  matrix products: 35.5 us -> 45.6 us
  starting transfers between devices: 9.87 us -> 0.13 us
  other arithmetic: 12.4 us -> 4.33 us
    all_to_all x2 -> x0, waiting for transfers between devices: 299 us -> none  [the longest x1 204 us: local(): lax.all_to_all(outgoing, ('node', 'local'), split_axis=0, concat_axis=0,...]
    reduce_scatter x0 -> x1, waiting for transfers between devices: none -> 95.6 us  [local(): combined = lax.psum_scatter(total, GROUP, scatter_dimension=0, tiled=True)]
    all_gather x0 -> x1, blocking collectives: none -> 33.7 us  [local(): coded = lax.all_gather(coded, GROUP, axis=0)]
    all_gather x2 -> x3, waiting for transfers between devices: 145 us -> 165 us  [the longest x2 127 us: gather_weight(): whole = lax.all_gather(piece, ('local', 'rep', 'node'), axis=0, tiled=True)]
    dot_general x0 -> x1, local copies, waits for them, and re-layouts: none -> 11.6 us  [local(): jnp.einsum('tl,clw->tcw', combined, up, preferred_element_type=jnp.float32)]
    dot_general x4 -> x6, matrix products: 35.5 us -> 45.6 us  [the longest x1 13.6 us: local(): answer = jnp.dot(hidden, expert_down[j], preferred_element_type=jnp.float32)]
    all_to_all x2 -> x0, starting transfers between devices: 9.64 us -> none  [the longest x1 4.96 us: local(): lax.all_to_all(answer.astype(jnp.bfloat16), ('node', 'local'), split_axis...]
    gather x1 -> x0, local copies, waits for them, and re-layouts: 8.73 us -> none  [local(): back_rows[target].reshape(tok_rows, top_k, latent_width).astype(jnp.float32)]
  transfers between devices with their start and end apart: 4 -> 4, of which waited for: 3 -> 4; matrix products, arithmetic and copies ran while one was open for 9% -> 13% of each run, Pallas kernels for 0% -> 0%
where the time goes in v1:
time: 374 us; the launch traced here: 373 us
  waiting for transfers between devices  260 us (70%)
  matrix products  45.6 us (12%)
  blocking collectives  33.7 us (9%)
  local copies, waits for them, and re-layouts  15.8 us (4%)
  between operations  13.2 us (4%)
  other arithmetic  4.33 us (1%)
    all_gather x2, waiting for transfers between devices, gather_weight(): whole = lax.all_gather(piece, ('local', 'rep', 'node'), axis=0, tiled=True)  127 us
    reduce_scatter x1, waiting for transfers between devices, local(): combined = lax.psum_scatter(total, GROUP, scatter_dimension=0, tiled=True)  95.6 us
    all_gather x1, waiting for transfers between devices, local(): everyone = lax.all_gather(latent, GROUP, axis=0)  37.4 us
    all_gather x1, blocking collectives, local(): coded = lax.all_gather(coded, GROUP, axis=0)  33.7 us
    dot_general x1, matrix products, local(): answer = jnp.dot(hidden, expert_down[j], preferred_element_type=jnp.float32)  13.6 us
    dot_general x1, local copies, waits for them, and re-layouts, local(): jnp.einsum('tl,clw->tcw', combined, up, preferred_element_type=jnp.float32)  11.6 us
    dot_general x1, matrix products, local(): jnp.einsum('tl,clw->tcw', combined, up, preferred_element_type=jnp.float32)  7.96 us
  transfers between devices with their start and end apart: 4, of which 4 were waited for; matrix products, arithmetic and copies ran while one was open for 13% of the time, Pallas kernels for 0%

profile of v1, /device:TPU:0, one launch (start us, length us, event | category | flops | bytes accessed | tf_op | source)
XLA Modules:
  0.0 373.2 jit_solution(15976843019126945014)
XLA Ops:
  6.5 0.0 copy-start
  6.5 0.0 all-gather.6.cloned.1.call-start
  6.5 1.6 copy-done
  8.1 0.7 constant_dynamic-slice_fusion.1
  8.8 0.0 all-gather.6.cloned.1.call-update
  8.9 0.0 all-gather.10.cloned.1.call-start
  8.9 2.1 fusion.1
  11.0 0.0 copy-start.3
  11.0 0.0 copy-start.4
  11.0 79.3 %all-gather.6.cloned.1.call-done = bf16[4096,1024]{1,0:T(8,128)(2,1)} async-done(((bf16[128,1024]{1,0:T(8,128)(2,1)}), bf16[4096,1024]{1,0:T(8,128)(2,1)}) %all-gather.6.cloned.1.call-update) | async-done | bytes 8388624 | tf_op jit(solution)/shard_map/all_gather | solution.py:14
  90.4 7.2 %fusion.11 = bf16[256,1024]{1,0:T(8,128)(2,1)} fusion(bf16[4096,1024]{1,0:T(8,128)(2,1)} %all-gather.6.cloned.1.call-done, bf16[256,4096]{1,0:T(8,128)(2,1)} %param.8, f32[256]{0:T(256)S(1)} %add_rsqrt_fusion), kind=kOutput, calls=%fused_computation.18 | convolution fusion | flops 2150891520 | bytes 11011072 | tf_op jit(solution)/shard_map/dot_general | solution.py:40
  97.6 0.0 all-gather.10.cloned.1.call-update
  97.6 0.0 all-gather.8.cloned.1.call-start
  97.6 1.7 constant_dynamic-slice_fusion
  99.3 0.0 all-gather.8.cloned.1.call-update
  99.4 0.0 reduce-scatter.2.cloned.1.call-start
  99.4 0.0 copy-done.3
  99.4 0.0 copy-done.4
  99.5 33.7 %all-gather = s32[128,256]{1,0:T(8,128)S(1)} all-gather(s32[8,256]{1,0:T(8,128)S(1)} %pad_add_fusion), channel_id=2, replica_groups=mesh['rep'=2,'node'=4,'local'=4] {'node','local'}, dimensions={0}, use_global_device_ids=true | all-gather | bytes 139264 | tf_op jit(solution)/shard_map/all_gather | solution.py:32
  133.1 0.1 fusion.18
  133.2 0.6 reduce-window.6
  133.8 0.2 slice_reduce_fusion
  134.0 0.1 fusion.16
  134.1 0.1 bitcast_select_fusion
  134.2 1.4 select_reduce_fusion
  135.6 37.4 %all-gather.10.cloned.1.call-done = bf16[4096,1024]{1,0:T(8,128)(2,1)} async-done(((bf16[256,1024]{1,0:T(8,128)(2,1)}), bf16[4096,1024]{1,0:T(8,128)(2,1)}) %all-gather.10.cloned.1.call-update) | async-done | bytes 8388624 | tf_op jit(solution)/shard_map/all_gather | solution.py:41
  173.0 0.0 copy-start.5
  173.0 4.7 %convolution_convert_fusion.1 = bf16[16,128,1024]{2,1,0:T(8,128)(2,1)S(1)} fusion(bf16[16,256,1024]{2,1,0:T(8,128)(2,1)} %bitcast.40, s32[16,256]{1,0:T(8,128)S(1)} %bitcast_select_fusion), kind=kOutput, calls=%fused_computation.9 | convolution fusion | flops 1076363264 | bytes 12599296 | tf_op jit(solution)/shard_map/sct,stl->scl/dot_general | solution.py:54
  177.7 0.0 copy-start.2
  177.7 0.0 copy-done.5
  177.7 5.4 %fusion.9 = f32[2048,768]{1,0:T(8,128)} fusion(bf16[2048,1024]{1,0:T(8,128)(2,1)S(1)} %bitcast.42, bf16[1,1024,768]{2,1,0:T(8,128)(2,1)S(1)} %copy-done.5), kind=kOutput, calls=%fused_computation.16 | convolution fusion | flops 3221225472 | bytes 12058624 | tf_op jit(solution)/shard_map/dot_general | solution.py:58
  183.1 0.0 copy-done.2
  183.1 13.6 %multiply_convert_fusion = bf16[2048,1024]{1,0:T(8,128)(2,1)} fusion(f32[2048]{0:T(1024)S(1)} %bitcast.48, f32[2048,768]{1,0:T(8,128)} %fusion.9, bf16[2048,1024]{1,0:T(8,128)(2,1)} %bitcast.43, bf16[1,768,1024]{2,1,0:T(8,128)(2,1)} %param.15, bf16[1,1024,768]{2,1,0:T(8,128)(2,1)} %param.14), kind=kOutput, calls=%fused_computation | convolution fusion | flops 6456082432 | bytes 17833984 | tf_op jit(solution)/shard_map/dot_general | solution.py:61
  196.7 6.8 %convolution_convert_fusion = bf16[16,256,1024]{2,1,0:T(8,128)(2,1)} fusion(bf16[16,128,1024]{2,1,0:T(8,128)(2,1)} %bitcast.41, s32[16,256]{1,0:T(8,128)S(1)} %bitcast_select_fusion), kind=kOutput, calls=%fused_computation.1 | convolution fusion | flops 1078460416 | bytes 12599296 | tf_op jit(solution)/shard_map/sct,scl->stl/dot_general | solution.py:63
  203.5 0.0 reduce-scatter.2.cloned.1.call-update
  203.5 48.1 %all-gather.8.cloned.1.call-done = bf16[4096,1024]{1,0:T(8,128)(2,1)} async-done(((bf16[128,1024]{1,0:T(8,128)(2,1)}), bf16[4096,1024]{1,0:T(8,128)(2,1)}) %all-gather.8.cloned.1.call-update) | async-done | bytes 8388624 | tf_op jit(solution)/shard_map/all_gather | solution.py:14
  251.6 11.6 %copy.16 = bf16[4,1024,1024]{2,1,0:T(8,128)(2,1)} copy(bf16[4,1024,1024]{1,2,0:T(8,128)(2,1)} %bitcast.44) | data formatting | bytes 16777216 | tf_op jit(solution)/shard_map/tl,clw->tcw/dot_general | solution.py:74
  263.2 95.6 %reduce-scatter.2.cloned.1.call-done = bf16[256,1024]{1,0:T(8,128)(2,1)} async-done(((bf16[4096,1024]{1,0:T(8,128)(2,1)}), bf16[256,1024]{1,0:T(8,128)(2,1)}) %reduce-scatter.2.cloned.1.call-update) | async-done | bytes 524304 | tf_op jit(solution)/shard_map/reduce_scatter | solution.py:71
  358.7 0.0 copy-start.1
  358.7 8.0 %fusion = bf16[256,4096]{1,0:T(8,128)(2,1)} fusion(bf16[256,1024]{1,0:T(8,128)(2,1)} %reduce-scatter.2.cloned.1.call-done, bf16[4096,1024]{1,0:T(8,128)(2,1)} %bitcast.45, bf16[256,4096]{1,0:T(8,128)(2,1)} %param.8), kind=kOutput, calls=%fused_computation.6 | convolution fusion | flops 2150629376 | bytes 13107200 | tf_op jit(solution)/shard_map/tl,clw->tcw/dot_general | solution.py:74
  366.7 0.0 copy-done.1
  (6 shorter events, 0.1 us)
Async XLA Ops:
  6.5 1.6 copy-start
  6.5 83.8 %all-gather.6.cloned.1.call-start = ((), (), s32[]{:S(2)}) async-start(), calls=%async_computation.1 | async-start | bytes 8650752 | tf_op jit(solution)/shard_map/all_gather | solution.py:14
  8.9 164.1 %all-gather.10.cloned.1.call-start = ((), (), s32[]{:S(2)}) async-start(), calls=%async_computation.4 | async-start | bytes 8912896 | tf_op jit(solution)/shard_map/all_gather | solution.py:41
  11.0 88.4 %copy-start.3 = (s32[256,4]{0,1:T(4,128)S(1)}, s32[256,4]{0,1:T(4,128)}, u32[]{:S(2)}) copy-start(s32[256,4]{0,1:T(4,128)} %param.10) | copy-start | bytes 12292
  11.0 88.4 %copy-start.4 = (s32[256,4]{0,1:T(4,128)S(1)}, s32[256,4]{0,1:T(4,128)}, u32[]{:S(2)}) copy-start(s32[256,4]{0,1:T(4,128)} %param.9) | copy-start | bytes 12292
  97.6 154.0 %all-gather.8.cloned.1.call-start = ((), (), s32[]{:S(2)}) async-start(), calls=%async_computation.3 | async-start | bytes 8650752 | tf_op jit(solution)/shard_map/all_gather | solution.py:14
  99.4 259.4 %reduce-scatter.2.cloned.1.call-start = ((), (), s32[]{:S(2)}) async-start(), calls=%async_computation.2 | async-start | bytes 8912896 | tf_op jit(solution)/shard_map/reduce_scatter | solution.py:71
  173.0 4.8 %copy-start.5 = (bf16[1,1024,768]{2,1,0:T(8,128)(2,1)S(1)}, bf16[1,1024,768]{2,1,0:T(8,128)(2,1)}, u32[]{:S(2)}) copy-start(bf16[1,1024,768]{2,1,0:T(8,128)(2,1)} %param.13) | copy-start | bytes 4718596
  177.7 5.4 %copy-start.2 = (bf16[16,128,1024]{2,1,0:T(8,128)(2,1)}, bf16[16,128,1024]{2,1,0:T(8,128)(2,1)S(1)}, u32[]{:S(2)}) copy-start(bf16[16,128,1024]{2,1,0:T(8,128)(2,1)S(1)} %convolution_convert_fusion.1) | copy-start | bytes 12582916
  358.7 8.0 %copy-start.1 = (bf16[1024,1024]{1,0:T(8,128)(2,1)S(1)}, bf16[1024,1024]{1,0:T(8,128)(2,1)}, u32[]{:S(2)}) copy-start(bf16[1024,1024]{1,0:T(8,128)(2,1)} %param.11) | copy-start | bytes 6291460
Sparse Core Ops, SparseCore 0:
  10.2 80.1 all-gather.5
  97.7 75.2 all-gather.9
  175.8 75.6 all-gather.7
  255.5 103.1 reduce-scatter.1

commit v2 on v1

--- a/solution.py
+++ b/solution.py
@@ -1,21 +1,83 @@
 import jax
 import jax.numpy as jnp
 from jax import lax
+from jax.experimental import pallas as pl
+from jax.experimental.pallas import tpu as pltpu
 from jax.sharding import PartitionSpec as P
 
 GROUP = ("node", "local")
 
 
-def gather_weight(w, axis):
-    copies = lax.axis_size("rep") * lax.axis_size("node")
-    part = w.shape[0] // copies
-    mine = lax.axis_index("rep") * lax.axis_size("node") + lax.axis_index("node")
-    piece = lax.dynamic_slice_in_dim(w, mine * part, part, axis=0)
-    whole = lax.all_gather(piece, ("local", "rep", "node"), axis=0, tiled=True)
-    if axis == 0:
-        return whole
-    n_local = lax.axis_size("local")
-    return whole.reshape(n_local, w.shape[0], w.shape[1])
+def gather_weight(w):
+    part = w.shape[0] // lax.axis_size("node")
+    piece = lax.dynamic_slice_in_dim(w, lax.axis_index("node") * part, part, axis=0)
+    return lax.all_gather(piece, GROUP, axis=0)
+
+
+def down_kernel(a_ref, w_ref, out_ref, total):
+    step = pl.program_id(0)
+
+    @pl.when(step == 0)
+    def _():
+        total[...] = jnp.zeros_like(total)
+
+    total[...] += jnp.dot(a_ref[...], w_ref[0], preferred_element_type=jnp.float32)
+
+    @pl.when(step == pl.num_programs(0) - 1)
+    def _():
+        out_ref[...] = total[...].astype(out_ref.dtype)
+
+
+def down_project(a, pieces):
+    n_node, n_local = lax.axis_size("node"), lax.axis_size("local")
+    steps, part, width = pieces.shape
+    ordered = a.reshape(a.shape[0], n_local, n_node, part).transpose(2, 1, 0, 3)
+    ordered = ordered.reshape(steps, a.shape[0], part)
+    return pl.pallas_call(
+        lambda a_ref, *rest: down_kernel(a_ref.at[0], *rest),
+        grid=(steps,),
+        out_shape=jax.ShapeDtypeStruct((a.shape[0], width), jnp.bfloat16),
+        in_specs=[
+            pl.BlockSpec((1, a.shape[0], part), lambda i: (i, 0, 0)),
+            pl.BlockSpec((1, part, width), lambda i: (i, 0, 0)),
+        ],
+        out_specs=pl.BlockSpec((a.shape[0], width), lambda i: (0, 0)),
+        scratch_shapes=[pltpu.VMEM((a.shape[0], width), jnp.float32)],
+        compiler_params=pltpu.CompilerParams(vmem_limit_bytes=24 * 2**20),
+    )(ordered, pieces)
+
+
+def up_kernel(a_ref, w_ref, tok_ref, out_ref, total):
+    step = pl.program_id(1)
+
+    @pl.when(step == 0)
+    def _():
+        total[...] = tok_ref[...].astype(jnp.float32)
+
+    total[...] += jnp.dot(a_ref[...], w_ref[0], preferred_element_type=jnp.float32)
+
+    @pl.when(step == pl.num_programs(1) - 1)
+    def _():
+        out_ref[...] = total[...].astype(out_ref.dtype)
+
+
+def up_project(a, pieces, tokens):
+    n_node, n_local = lax.axis_size("node"), lax.axis_size("local")
+    _, part, columns = pieces.shape
+    rows = a.shape[0]
+    return pl.pallas_call(
+        up_kernel,
+        grid=(n_local, n_node),
+        out_shape=jax.ShapeDtypeStruct(tokens.shape, jnp.bfloat16),
+        in_specs=[
+            pl.BlockSpec((rows, part), lambda c, k: (0, k)),
+            pl.BlockSpec((1, part, columns), lambda c, k: (k * n_local + c, 0, 0)),
+            pl.BlockSpec((rows, columns), lambda c, k: (0, c)),
+        ],
+        out_specs=pl.BlockSpec((rows, columns), lambda c, k: (0, c)),
+        scratch_shapes=[pltpu.VMEM((rows, columns), jnp.float32)],
+        compiler_params=pltpu.CompilerParams(vmem_limit_bytes=24 * 2**20),
+    )(a, pieces, tokens)
 
 
 def local(tokens, routes, gates, w_down, w_up, expert_gate, expert_up, expert_down):
@@ -28,17 +90,21 @@
     capacity = 2 * tok_rows * top_k // experts_all
     me = lax.axis_index("node") * lax.axis_size("local") + lax.axis_index("local")
 
-    coded = jnp.concatenate([routes.T, gates.T], axis=0)
-    coded = lax.all_gather(coded, GROUP, axis=0)
-    all_routes, all_gates = coded[:, :top_k], coded[:, top_k:]
+    coded = jnp.stack([routes.T, gates.T // 256, gates.T % 256]).astype(jnp.bfloat16)
+    code_rows = -(-coded.size // (16 * width)) * 16
+    coded = jnp.pad(coded.reshape(-1), (0, code_rows * width - coded.size))
+    coded = coded.reshape(code_rows, width)
 
     tok32 = tokens.astype(jnp.float32)
     normed = (tok32 * lax.rsqrt(jnp.mean(tok32 * tok32, axis=-1, keepdims=True) + 1e-06)).astype(
         jnp.bfloat16
     )
-    down = gather_weight(w_down, 0)
-    latent = jnp.dot(normed, down, preferred_element_type=jnp.float32).astype(jnp.bfloat16)
-    everyone = lax.all_gather(latent, GROUP, axis=0)
+    latent = down_project(normed, gather_weight(w_down))
+    everyone = lax.all_gather(jnp.concatenate([latent, coded]), GROUP, axis=0)
+    codes = everyone[:, tok_rows:].reshape(owners, -1)[:, : 3 * top_k * tok_rows]
+    codes = codes.astype(jnp.int32).reshape(owners, 3, top_k, tok_rows)
+    all_routes = codes[:, 0]
+    all_gates = codes[:, 1] * 256 + codes[:, 2]
 
     total = None
     for j in range(exp_local):
@@ -51,8 +117,10 @@
         pick = rank[:, None, :] == jnp.arange(capacity, dtype=jnp.int32)[None, :, None]
         pick16 = pick.astype(jnp.bfloat16)
         row_weight = jnp.sum(jnp.where(pick, weight[:, None, :], 0.0), axis=2)
+        longer = jnp.pad(rank, ((0, 0), (0, code_rows)), constant_values=-1)
+        longer = longer[:, None, :] == jnp.arange(capacity, dtype=jnp.int32)[None, :, None]
         rows = jnp.einsum(
-            "sct,stl->scl", pick16, everyone, preferred_element_type=jnp.float32
+            "sct,stl->scl", longer.astype(jnp.bfloat16), everyone, preferred_element_type=jnp.float32
         ).astype(jnp.bfloat16)
         rows = rows.reshape(owners * capacity, width)
         gate = jnp.dot(rows, expert_gate[j], preferred_element_type=jnp.float32)
@@ -70,9 +138,7 @@
     total = total.astype(jnp.bfloat16).reshape(owners * tok_rows, width)
     combined = lax.psum_scatter(total, GROUP, scatter_dimension=0, tiled=True)
 
-    up = gather_weight(w_up, 1)
-    product = jnp.einsum("tl,clw->tcw", combined, up, preferred_element_type=jnp.float32)
-    return (tok32 + product.reshape(tok_rows, -1)).astype(jnp.bfloat16)
+    return up_project(combined, gather_weight(w_up), tokens)
 
 
 def solution(mesh):

time: 374 us -> 377 us (level)
  blocking collectives: 33.7 us -> 0 us
  waiting for transfers between devices: 260 us -> 288 us
  Pallas kernels: 0 us -> 13.2 us
  matrix products: 45.6 us -> 33 us
  local copies, waits for them, and re-layouts: 15.8 us -> 20.7 us
    all_gather x1 -> x0, blocking collectives: 33.7 us -> none  [local(): coded = lax.all_gather(coded, GROUP, axis=0)]
    all_gather x3, waiting for transfers between devices: 165 us -> 181 us  [the longest x2 107 us: gather_weight(): return lax.all_gather(piece, GROUP, axis=0)]
    pallas_call x0 -> x2, Pallas kernels: none -> 13.2 us  [the longest x1 8.08 us: up_project(): pl.pallas_call(up_kernel, grid=(n_local, n_node), out_shape=jax.ShapeDtyp...]
    dot_general x3 -> x1, matrix products: 19.9 us -> 7.38 us  [local(): jnp.einsum('sct,stl->scl', longer.astype(jnp.bfloat16), everyone, preferr...]
    dot_general x1 -> x0, local copies, waits for them, and re-layouts: 11.6 us -> none  [local(): jnp.einsum('tl,clw->tcw', combined, up, preferred_element_type=jnp.float32)]
    reduce_scatter x1, waiting for transfers between devices: 95.6 us -> 107 us  [local(): combined = lax.psum_scatter(total, GROUP, scatter_dimension=0, tiled=True)]
    unnamed x12 -> x22, local copies, waits for them, and re-layouts: 1.61 us -> 11.5 us
    reshape x0 -> x4, local copies, waits for them, and re-layouts: none -> 5.17 us  [the longest x2 5.06 us: down_project(): ordered = a.reshape(a.shape[0], n_local, n_node, part).transpose(2, 1, 0, 3)]
where the time goes in v2:
time: 377 us; the launch traced here: 376 us
  waiting for transfers between devices  288 us (76%)
  matrix products  33 us (9%)
  local copies, waits for them, and re-layouts  20.7 us (5%)
  between operations  13.3 us (4%)
  Pallas kernels  13.2 us (4%)
  other arithmetic  7.43 us (2%)
    reduce_scatter x1, waiting for transfers between devices, local(): combined = lax.psum_scatter(total, GROUP, scatter_dimension=0, tiled=True)  107 us
    all_gather x2, waiting for transfers between devices, gather_weight(): return lax.all_gather(piece, GROUP, axis=0)  107 us
    all_gather x1, waiting for transfers between devices, local(): everyone = lax.all_gather(jnp.concatenate([latent, coded]), GROUP, axis=0)  74.4 us
    dot_general x1, matrix products, local(): answer = jnp.dot(hidden, expert_down[j], preferred_element_type=jnp.float32)  13.5 us
    unnamed x22, local copies, waits for them, and re-layouts  11.5 us
    pallas_call x1, Pallas kernels, up_project(): pl.pallas_call(up_kernel, grid=(n_local, n_node), out_shape=jax.ShapeDtyp...  8.08 us
  transfers between devices with their start and end apart: 4, of which 4 were waited for; matrix products, arithmetic and copies ran while one was open for 13% of the time, Pallas kernels for 0%

profile of v2, /device:TPU:0, one launch (start us, length us, event | category | flops | bytes accessed | tf_op | source)
XLA Modules:
  0.0 376.2 jit_solution(706823578295445887)
XLA Ops:
  6.5 0.0 copy-start
  6.5 0.0 all-gather.7.cloned.1.call-start
  6.5 1.6 copy-done
  8.1 0.9 constant_dynamic-slice_fusion.1
  9.0 0.0 all-gather.7.cloned.1.call-update
  9.0 0.0 all-gather.9.cloned.1.call-start
  9.1 2.1 fusion
  11.2 2.2 fusion.1
  13.4 0.0 copy-start.7
  13.4 0.0 copy-start.8
  13.4 2.8 reshape.78
  16.2 2.3 copy.10
  18.5 0.0 copy-done.7
  18.5 0.0 copy-done.8
  18.6 68.6 %all-gather.7.cloned.1.call-done = bf16[4096,1024]{1,0:T(8,128)(2,1)} async-done(((bf16[256,1024]{1,0:T(8,128)(2,1)}), bf16[4096,1024]{1,0:T(8,128)(2,1)}) %all-gather.7.cloned.1.call-update) | async-done | bytes 8388624 | tf_op jit(solution)/shard_map/all_gather | solution.py:14
  87.2 3.4 copy-done.4
  90.6 5.1 %shard_map.82 = bf16[256,1024]{1,0:T(8,128)(2,1)S(1)} custom-call(bf16[16,256,256]{2,1,0:T(8,128)(2,1)S(1)} %bitcast.73, bf16[16,256,1024]{2,1,0:T(8,128)(2,1)S(1)} %bitcast.72), custom_call_target="tpu_custom_call" | custom-call | tf_op jit(solution)/shard_map/pallas_call | solution.py:36
  95.7 0.8 pad_maximum_fusion
  96.5 0.0 all-gather.9.cloned.1.call-update
  96.5 0.0 all-gather.11.cloned.1.call-start
  96.6 1.9 constant_dynamic-slice_fusion
  98.5 0.0 all-gather.11.cloned.1.call-update
  98.5 0.2 reduce-scatter.2.cloned.1.call-start
  98.8 74.4 %all-gather.9.cloned.1.call-done = bf16[4352,1024]{1,0:T(8,128)(2,1)} async-done(((bf16[272,1024]{1,0:T(8,128)(2,1)}), bf16[4352,1024]{1,0:T(8,128)(2,1)}) %all-gather.9.cloned.1.call-update) | async-done | bytes 8912912 | tf_op jit(solution)/shard_map/all_gather | solution.py:103
  173.2 1.1 slice.28
  174.2 0.3 copy.16
  174.6 0.1 reshape.89
  174.7 0.1 fusion.18
  174.8 0.6 reduce-window.6
  175.3 0.2 slice_reduce_fusion
  175.6 0.1 bitcast_select_fusion
  175.7 0.1 fusion.10
  175.7 1.4 select_reduce_fusion
  177.2 0.0 copy-start.9
  177.2 7.4 %convolution_convert_fusion.1 = bf16[16,128,1024]{2,1,0:T(8,128)(2,1)S(1)} fusion(bf16[16,272,1024]{2,1,0:T(8,128)(2,1)} %bitcast.76, s32[16,272]{1,0:T(8,128)S(1)} %pad.9), kind=kOutput, calls=%fused_computation.7 | convolution fusion | flops 1143504896 | bytes 13124608 | tf_op jit(solution)/shard_map/sct,stl->scl/dot_general | solution.py:122
  184.6 0.0 copy-start.6
  184.6 0.0 copy-done.9
  184.6 5.3 %fusion.5 = f32[2048,768]{1,0:T(8,128)} fusion(bf16[2048,1024]{1,0:T(8,128)(2,1)S(1)} %bitcast.78, bf16[1,1024,768]{2,1,0:T(8,128)(2,1)S(1)} %copy-done.9), kind=kOutput, calls=%fused_computation.13 | convolution fusion | flops 3221225472 | bytes 12058624 | tf_op jit(solution)/shard_map/dot_general | solution.py:126
  189.9 0.0 copy-done.6
  189.9 13.5 %multiply_convert_fusion = bf16[2048,1024]{1,0:T(8,128)(2,1)} fusion(f32[2048]{0:T(1024)S(1)} %bitcast.83, f32[2048,768]{1,0:T(8,128)} %fusion.5, bf16[2048,1024]{1,0:T(8,128)(2,1)} %bitcast.79, bf16[1,768,1024]{2,1,0:T(8,128)(2,1)} %param.15, bf16[1,1024,768]{2,1,0:T(8,128)(2,1)} %param.14), kind=kOutput, calls=%fused_computation | convolution fusion | flops 6456082432 | bytes 17833984 | tf_op jit(solution)/shard_map/dot_general | solution.py:129
  203.4 6.8 %convolution_convert_fusion = bf16[16,256,1024]{2,1,0:T(8,128)(2,1)} fusion(bf16[16,128,1024]{2,1,0:T(8,128)(2,1)} %bitcast.77, s32[16,256]{1,0:T(8,128)S(1)} %bitcast_select_fusion), kind=kOutput, calls=%fused_computation.1 | convolution fusion | flops 1078460416 | bytes 12599296 | tf_op jit(solution)/shard_map/sct,scl->stl/dot_general | solution.py:131
  210.2 0.0 reduce-scatter.2.cloned.1.call-update
  210.3 38.2 %all-gather.11.cloned.1.call-done = bf16[4096,1024]{1,0:T(8,128)(2,1)} async-done(((bf16[256,1024]{1,0:T(8,128)(2,1)}), bf16[4096,1024]{1,0:T(8,128)(2,1)}) %all-gather.11.cloned.1.call-update) | async-done | bytes 8388624 | tf_op jit(solution)/shard_map/all_gather | solution.py:14
  248.5 106.9 %reduce-scatter.2.cloned.1.call-done.a_ref = bf16[256,1024]{1,0:T(8,128)(2,1)} async-done(((bf16[4096,1024]{1,0:T(8,128)(2,1)}), bf16[256,1024]{1,0:T(8,128)(2,1)}) %reduce-scatter.2.cloned.1.call-update) | async-done | bytes 524304 | tf_op jit(solution)/shard_map/reduce_scatter | solution.py:139
  355.4 1.7 copy-done.2
  357.2 3.4 copy-done.3
  360.6 1.0 copy-done.5
  361.6 8.1 %shard_map.83 = bf16[256,4096]{1,0:T(8,128)(2,1)} custom-call(bf16[256,1024]{1,0:T(8,128)(2,1)S(1)} %copy-done.5, bf16[16,256,1024]{2,1,0:T(8,128)(2,1)S(1)} %bitcast.71, bf16[256,4096]{1,0:T(8,128)(2,1)S(1)} %copy-done.2), custom_call_target="tpu_custom_call" | custom-call | tf_op jit(solution)/shard_map/pallas_call | solution.py:68
  (19 shorter events, 0.2 us)
Async XLA Ops:
  6.5 1.6 copy-start
  6.5 80.7 %all-gather.7.cloned.1.call-start = ((), (), s32[]{:S(2)}) async-start(), calls=%async_computation.2 | async-start | bytes 8912896 | tf_op jit(solution)/shard_map/all_gather | solution.py:14
  9.0 164.1 %all-gather.9.cloned.1.call-start = ((), (), s32[]{:S(2)}) async-start(), calls=%async_computation.3 | async-start | bytes 9469952 | tf_op jit(solution)/shard_map/all_gather | solution.py:103
  13.4 5.1 %copy-start.7 = (s32[256,4]{0,1:T(4,128)S(1)}, s32[256,4]{0,1:T(4,128)}, u32[]{:S(2)}) copy-start(s32[256,4]{0,1:T(4,128)} %param.9) | copy-start | bytes 12292
  13.4 5.1 %copy-start.8 = (s32[256,4]{0,1:T(4,128)S(1)}, s32[256,4]{0,1:T(4,128)}, u32[]{:S(2)}) copy-start(s32[256,4]{0,1:T(4,128)} %param.10) | copy-start | bytes 12292
  87.2 3.4 copy-start.4
  96.5 152.0 %all-gather.11.cloned.1.call-start = ((), (), s32[]{:S(2)}) async-start(), calls=%async_computation.4 | async-start | bytes 8912896 | tf_op jit(solution)/shard_map/all_gather | solution.py:14
  98.5 256.9 %reduce-scatter.2.cloned.1.call-start = ((), (), s32[]{:S(2)}) async-start(), calls=%async_computation.1 | async-start | bytes 8912896 | tf_op jit(solution)/shard_map/reduce_scatter | solution.py:139
  177.2 7.4 %copy-start.9 = (bf16[1,1024,768]{2,1,0:T(8,128)(2,1)S(1)}, bf16[1,1024,768]{2,1,0:T(8,128)(2,1)}, u32[]{:S(2)}) copy-start(bf16[1,1024,768]{2,1,0:T(8,128)(2,1)} %param.13) | copy-start | bytes 4718596
  184.6 5.3 %copy-start.6 = (bf16[16,128,1024]{2,1,0:T(8,128)(2,1)}, bf16[16,128,1024]{2,1,0:T(8,128)(2,1)S(1)}, u32[]{:S(2)}) copy-start(bf16[16,128,1024]{2,1,0:T(8,128)(2,1)S(1)} %convolution_convert_fusion.1) | copy-start | bytes 12582916
  355.4 14.3 %copy-start.1 = (bf16[1024,1024]{1,0:T(8,128)(2,1)S(1)}, bf16[1024,1024]{1,0:T(8,128)(2,1)}, u32[]{:S(2)}) copy-start(bf16[1024,1024]{1,0:T(8,128)(2,1)} %param.11) | copy-start | bytes 6291460
  355.4 1.7 copy-start.2
  357.2 3.4 copy-start.3
  360.6 1.0 copy-start.5
Sparse Core Ops, SparseCore 0:
  9.6 77.5 all-gather.6
  96.7 76.4 all-gather.8
  175.4 73.0 all-gather.10
  252.4 102.9 reduce-scatter.1

commit v3 on v2

v3 whole, which is shorter than its diff:
```python
import jax
import jax.numpy as jnp
from jax import lax
from jax.experimental import pallas as pl
from jax.experimental.pallas import tpu as pltpu
from jax.sharding import PartitionSpec as P

GROUP = ("nx", "local")
PAIR = [(0, 1), (1, 0)]


def swap(x):
    return lax.ppermute(x, "core", PAIR)


def by_core(mine, theirs, axis):
    first = lax.axis_index("core") == 0
    return jnp.concatenate(
        [jnp.where(first, mine, theirs), jnp.where(first, theirs, mine)], axis=axis
    )


def gather_weight(w):
    part, half = w.shape[0] // lax.axis_size("nx"), w.shape[1] // 2
    start = (lax.axis_index("nx") * part, lax.axis_index("core") * half)
    return lax.all_gather(lax.dynamic_slice(w, start, (part, half)), GROUP, axis=0)


def down_kernel(a_ref, w_ref, out_ref, total):
    step = pl.program_id(0)

    @pl.when(step == 0)
    def _():
        total[...] = jnp.zeros_like(total)

    total[...] += jnp.dot(a_ref[...], w_ref[0], preferred_element_type=jnp.float32)

    @pl.when(step == pl.num_programs(0) - 1)
    def _():
        out_ref[...] = total[...].astype(out_ref.dtype)


def down_project(a, pieces):
    n_node, n_local = lax.axis_size("nx"), lax.axis_size("local")
    steps, part, width = pieces.shape
    ordered = a.reshape(a.shape[0], n_local, n_node, part).transpose(2, 1, 0, 3)
    ordered = ordered.reshape(steps, a.shape[0], part)
    return pl.pallas_call(
        lambda a_ref, *rest: down_kernel(a_ref.at[0], *rest),
        grid=(steps,),
        out_shape=jax.ShapeDtypeStruct((a.shape[0], width), jnp.bfloat16),
        in_specs=[
            pl.BlockSpec((1, a.shape[0], part), lambda i: (i, 0, 0)),
            pl.BlockSpec((1, part, width), lambda i: (i, 0, 0)),
        ],
        out_specs=pl.BlockSpec((a.shape[0], width), lambda i: (0, 0)),
        scratch_shapes=[pltpu.VMEM((a.shape[0], width), jnp.float32)],
        compiler_params=pltpu.CompilerParams(vmem_limit_bytes=24 * 2**20),
    )(ordered, pieces)


def up_kernel(a_ref, w_ref, tok_ref, out_ref, total):
    step = pl.program_id(1)

    @pl.when(step == 0)
    def _():
        total[...] = tok_ref[...].astype(jnp.float32)

    total[...] += jnp.dot(a_ref[...], w_ref[0], preferred_element_type=jnp.float32)

    @pl.when(step == pl.num_programs(1) - 1)
    def _():
        out_ref[...] = total[...].astype(out_ref.dtype)


def up_project(a, pieces, tokens):
    n_node, n_local = lax.axis_size("nx"), lax.axis_size("local")
    _, part, columns = pieces.shape
    rows = a.shape[0]
    return pl.pallas_call(
        up_kernel,
        grid=(n_local, n_node),
        out_shape=jax.ShapeDtypeStruct(tokens.shape, jnp.bfloat16),
        in_specs=[
            pl.BlockSpec((rows, part), lambda c, k: (0, k)),
            pl.BlockSpec((1, part, columns), lambda c, k: (k * n_local + c, 0, 0)),
            pl.BlockSpec((rows, columns), lambda c, k: (0, c)),
        ],
        out_specs=pl.BlockSpec((rows, columns), lambda c, k: (0, c)),
        scratch_shapes=[pltpu.VMEM((rows, columns), jnp.float32)],
        compiler_params=pltpu.CompilerParams(vmem_limit_bytes=24 * 2**20),
    )(a, pieces, tokens)


def local(tokens, routes, gates, w_down, w_up, expert_gate, expert_up, expert_down):
    tok_rows, model = tokens.shape
    top_k = routes.shape[1]
    n_local = lax.axis_size("local")
    chips = lax.axis_size("nx") * n_local
    exp_local = expert_gate.shape[0]
    width = w_down.shape[1]
    half = width // 2
    capacity = 2 * tok_rows * top_k // (2 * chips * exp_local)
    core = lax.axis_index("core")

    codes = jnp.concatenate([routes.T, gates.T], axis=0)
    codes = jnp.stack([codes, swap(codes)])
    coded = jnp.concatenate(
        [codes[:, :top_k], codes[:, top_k:] // 256, codes[:, top_k:] % 256], axis=1
    ).astype(jnp.bfloat16)
    code_size = coded.size
    code_rows = -(-code_size // (16 * half)) * 16
    coded = jnp.pad(coded.reshape(-1), (0, code_rows * half - code_size))
    coded = coded.reshape(code_rows, half)

    both = jnp.concatenate([tokens, swap(tokens)], axis=0)
    both32 = both.astype(jnp.float32)
    normed = (
        both32 * lax.rsqrt(jnp.mean(both32 * both32, axis=-1, keepdims=True) + 1e-06)
    ).astype(jnp.bfloat16)
    latent = down_project(normed, gather_weight(w_down))
    gathered = lax.all_gather(jnp.concatenate([latent, coded]), GROUP, axis=0)
    everyone = gathered[:, : 2 * tok_rows].reshape(chips, 2, tok_rows, half)
    codes = gathered[:, 2 * tok_rows :].reshape(chips, -1)[:, :code_size]
    codes = codes.astype(jnp.int32).reshape(chips, 2, 3, top_k, tok_rows)
    all_routes = codes[:, :, 0]
    all_gates = codes[:, :, 1] * 256 + codes[:, :, 2]

    def owner(which):
        node = lax.axis_index("nx") * 2 + which
        return (node * n_local + lax.axis_index("local")) * exp_local

    def find(expert):
        named = all_routes == expert
        mask = jnp.any(named, axis=2)
        weight = jnp.sum(jnp.where(named, all_gates, 0), axis=2)
        rank = jnp.where(mask, jnp.cumsum(mask.astype(jnp.int32), axis=2) - 1, -1)
        pick = rank[:, :, None, :] == jnp.arange(capacity, dtype=jnp.int32)[None, None, :, None]
        return pick, weight.astype(jnp.float32) * (1.0 / 32768.0)

    total = None
    for j in range(exp_local):
        pick, weight = find(owner(core) + j)
        pick_other, _ = find(owner(1 - core) + j)
        picks = jnp.concatenate([pick, pick_other], axis=2).astype(jnp.bfloat16)
        row_weight = jnp.sum(jnp.where(pick, weight[:, :, None, :], 0.0), axis=3)
        sent = jnp.einsum(
            "spct,sptl->spcl",
            pick_other.astype(jnp.bfloat16),
            everyone,
            preferred_element_type=jnp.float32,
        ).astype(jnp.bfloat16)
        theirs = swap(sent[:, ::-1])
        mine = jnp.einsum(
            "spct,sptl->spcl",
            pick.astype(jnp.bfloat16),
            everyone,
            preferred_element_type=jnp.float32,
        ).astype(jnp.bfloat16)
        rows = by_core(mine, theirs, 3).reshape(2 * chips * capacity, width)
        gate = jnp.dot(rows, expert_gate[j], preferred_element_type=jnp.float32)
        upper = jnp.dot(rows, expert_up[j], preferred_element_type=jnp.float32)
        hidden = (jax.nn.silu(gate) * upper).astype(jnp.bfloat16)
        answer = jnp.dot(hidden, expert_down[j], preferred_element_type=jnp.float32)
        answer = (answer * row_weight.reshape(-1, 1)).astype(jnp.bfloat16)
        answer = answer.reshape(chips, 2, capacity, width)
        away = lax.dynamic_slice_in_dim(answer, (1 - core) * half, half, axis=3)
        kept = lax.dynamic_slice_in_dim(answer, core * half, half, axis=3)
        answers = jnp.concatenate([kept, swap(away[:, ::-1])], axis=2)
        placed = jnp.einsum("spct,spcl->sptl", picks, answers, preferred_element_type=jnp.float32)
        total = placed if total is None else total + placed
    total = total.astype(jnp.bfloat16).reshape(chips * 2 * tok_rows, half)
    combined = lax.psum_scatter(total, GROUP, scatter_dimension=0, tiled=True)
    turned = jnp.concatenate([combined[tok_rows:], combined[:tok_rows]])
    combined = by_core(combined, swap(turned), 1)

    columns = w_up.shape[1] // 2
    residual = both.reshape(2 * tok_rows, n_local, 2, columns)
    residual = lax.dynamic_index_in_dim(residual, core, axis=2, keepdims=False)
    mixed = up_project(combined, gather_weight(w_up), residual.reshape(2 * tok_rows, -1))
    mixed = mixed.reshape(2, tok_rows, n_local, 1, columns)
    return by_core(mixed[0], swap(mixed[1]), 2).reshape(tok_rows, model)


def solution(mesh):
    shape = mesh.shape
    split = (shape["rep"], shape["node"] // 2, 2, shape["local"])
    mesh = jax.sharding.Mesh(mesh.devices.reshape(split), ("rep", "nx", "core", "local"))
    return jax.shard_map(
        local,
        mesh=mesh,
        in_specs=(
            P(("rep", "nx", "core", "local"), None),
            P(("rep", "nx", "core", "local"), None),
            P(("rep", "nx", "core", "local"), None),
            P("local", None),
            P(None, "local"),
            P(("nx", "core", "local"), None, None),
            P(("nx", "core", "local"), None, None),
            P(("nx", "core", "local"), None, None),
        ),
        out_specs=P(("rep", "nx", "core", "local"), None),
        check_vma=False,
    )
```

time: 377 us -> 417 us (1.11)
  local copies, waits for them, and re-layouts: 20.7 us -> 82.7 us
  waiting for transfers between devices: 288 us -> 263 us
  other arithmetic: 7.43 us -> 15.1 us
  Pallas kernels: 13.2 us -> 8.43 us
    reduce_scatter x1, waiting for transfers between devices: 107 us -> 84.3 us  [local(): combined = lax.psum_scatter(total, GROUP, scatter_dimension=0, tiled=True)]
    concatenate x0 -> x6, local copies, waits for them, and re-layouts: none -> 22.5 us  [the longest x5 17.9 us: local(): both = jnp.concatenate([tokens, swap(tokens)], axis=0)]
    dynamic_slice x2 -> x4, local copies, waits for them, and re-layouts: 2.81 us -> 22.2 us  [the longest x1 14.3 us: local(): residual = lax.dynamic_index_in_dim(residual, core, axis=2, keepdims=False)]
    all_gather x3, waiting for transfers between devices: 181 us -> 173 us  [the longest x2 99.5 us: gather_weight(): lax.all_gather(lax.dynamic_slice(w, start, (part, half)), GROUP, axis=0)]
    reshape x4 -> x3, local copies, waits for them, and re-layouts: 5.17 us -> 12.3 us  [the longest x1 7.86 us: local(): residual = both.reshape(2 * tok_rows, n_local, 2, columns)]
    ppermute x0 -> x6, waiting for transfers between devices: none -> 6.48 us  [swap(): return lax.ppermute(x, 'core', PAIR)]
    rev x0 -> x2, local copies, waits for them, and re-layouts: none -> 4.61 us  [the longest x1 3.08 us: local(): theirs = swap(sent[:, ::-1])]
    slice x2 -> x6, local copies, waits for them, and re-layouts: 1.27 us -> 5.81 us  [the longest x1 4.43 us: local(): everyone = gathered[:, :2 * tok_rows].reshape(chips, 2, tok_rows, half)]
  transfers between devices with their start and end apart: 4 -> 10, of which waited for: 4 -> 7; matrix products, arithmetic and copies ran while one was open for 13% -> 14% of each run, Pallas kernels for 0% -> 0%
where the time goes in v3:
time: 417 us; the launch traced here: 416 us
  waiting for transfers between devices  263 us (63%)
  local copies, waits for them, and re-layouts  82.7 us (20%)
  matrix products  31.5 us (8%)
  other arithmetic  15.1 us (4%)
  between operations  13.5 us (3%)
  Pallas kernels  8.43 us (2%)
    all_gather x2, waiting for transfers between devices, gather_weight(): lax.all_gather(lax.dynamic_slice(w, start, (part, half)), GROUP, axis=0)  99.5 us
    reduce_scatter x1, waiting for transfers between devices, local(): combined = lax.psum_scatter(total, GROUP, scatter_dimension=0, tiled=True)  84.3 us
    all_gather x1, waiting for transfers between devices, local(): gathered = lax.all_gather(jnp.concatenate([latent, coded]), GROUP, axis=0)  73.2 us
    concatenate x5, local copies, waits for them, and re-layouts, local(): both = jnp.concatenate([tokens, swap(tokens)], axis=0)  17.9 us
    dynamic_slice x1, local copies, waits for them, and re-layouts, local(): residual = lax.dynamic_index_in_dim(residual, core, axis=2, keepdims=False)  14.3 us
    dot_general x1, matrix products, local(): answer = jnp.dot(hidden, expert_down[j], preferred_element_type=jnp.float32)  13.1 us
    unnamed x22, local copies, waits for them, and re-layouts  12.6 us
  transfers between devices with their start and end apart: 10, of which 7 were waited for; matrix products, arithmetic and copies ran while one was open for 14% of the time, Pallas kernels for 0%

profile of v3, /device:TPU:0, one launch (start us, length us, event | category | flops | bytes accessed | tf_op | source)
XLA Modules:
  0.0 415.9 jit_solution(12108039510756575770)
XLA Ops:
  6.5 2.0 dynamic_slice.16
  9.2 0.7 fusion.28
  9.9 3.1 constant_dynamic-update-slice_fusion.1
  13.1 4.5 %concatenate.38 = bf16[256,4,2,512]{3,2,1,0:T(2,128)(2,1)} reshape(bf16[256,4096]{1,0:T(8,128)(2,1)} %param.8) | data formatting | bytes 4194304 | tf_op jit(solution)/shard_map/concatenate | solution.py:116
  17.6 3.6 copy.35
  21.3 4.5 %concatenate.39 = bf16[256,4,2,512]{3,2,1,0:T(2,128)(2,1)} reshape(bf16[256,4096]{1,0:T(8,128)(2,1)} %collective-permute-done) | data formatting | bytes 4194304 | tf_op jit(solution)/shard_map/concatenate | solution.py:116
  25.8 2.3 copy.36
  28.0 3.1 constant_dynamic-update-slice_fusion
  31.2 3.3 multiply_reduce_fusion
  34.4 2.4 multiply_convert_fusion.1
  36.9 48.7 %all-gather.7.cloned.1.call-done = bf16[4096,512]{1,0:T(8,128)(2,1)} async-done(((bf16[512,512]{1,0:T(8,128)(2,1)}), bf16[4096,512]{1,0:T(8,128)(2,1)}) %all-gather.7.cloned.1.call-update) | async-done | bytes 4194320 | tf_op jit(solution)/shard_map/all_gather | solution.py:26
  85.6 2.2 copy-done.2
  87.8 2.2 copy-done.3
  90.0 3.7 shard_map.82
  93.7 0.8 pad_maximum_fusion.3
  94.8 73.2 %all-gather.9.cloned.1.call-done = bf16[4224,512]{1,0:T(8,128)(2,1)} async-done(((bf16[528,512]{1,0:T(8,128)(2,1)}), bf16[4224,512]{1,0:T(8,128)(2,1)}) %all-gather.9.cloned.1.call-update) | async-done | bytes 4325392 | tf_op jit(solution)/shard_map/all_gather | solution.py:122
  168.0 0.9 slice_bitcast_fusion
  168.9 4.4 %slice.77 = bf16[8,512,512]{2,1,0:T(8,128)(2,1)} slice(bf16[8,528,512]{2,1,0:T(8,128)(2,1)} %bitcast.71), slice={[0:8], [0:512], [0:512]} | slice | bytes 8388608 | tf_op jit(solution)/shard_map/slice | solution.py:123
  173.5 1.2 reduce-window.16
  175.0 4.5 %convolution_convert_fusion = bf16[8,2,128,512]{3,2,1,0:T(8,128)(2,1)} fusion(bf16[8,2,256,512]{3,2,1,0:T(8,128)(2,1)} %bitcast.67, s32[8,2,256]{2,1,0:T(2,128)S(1)} %copy.46), kind=kOutput, calls=%fused_computation.20 | convolution fusion | flops 538443776 | bytes 6307840 | tf_op jit(solution)/shard_map/spct,sptl->spcl/dot_general | solution.py:147
  179.4 3.1 rev.6
  182.5 1.1 reduce-window.14
  184.0 1.4 select_reduce_fusion
  185.5 1.6 collective-permute-done.2
  187.0 3.8 broadcast_select_fusion.1
  191.4 0.8 copy-done.8
  192.2 5.3 %fusion.15 = f32[2048,768]{1,0:T(8,128)} fusion(bf16[2048,1024]{1,0:T(8,128)(2,1)S(1)} %bitcast.75, bf16[1,1024,768]{2,1,0:T(8,128)(2,1)S(1)} %copy-done.8), kind=kOutput, calls=%fused_computation.24 | convolution fusion | flops 3221225472 | bytes 12058624 | tf_op jit(solution)/shard_map/dot_general | solution.py:161
  197.5 13.1 %multiply_convert_fusion = bf16[2048,1024]{1,0:T(8,128)(2,1)} fusion(f32[2048]{0:T(1024)S(1)} %bitcast.84, f32[2048,768]{1,0:T(8,128)} %fusion.15, bf16[2048,1024]{1,0:T(8,128)(2,1)} %bitcast.76, bf16[1,768,1024]{2,1,0:T(8,128)(2,1)S(1)} %copy-done, bf16[1,1024,768]{2,1,0:T(8,128)(2,1)} %param.14), kind=kOutput, calls=%fused_computation | convolution fusion | flops 6456082432 | bytes 17833984 | tf_op jit(solution)/shard_map/dot_general | solution.py:164
  210.6 3.9 constant_dynamic-slice_fusion.1
  214.5 1.5 rev.7
  216.2 0.7 iota_compare_fusion
  216.9 0.7 iota_compare_fusion.1
  217.6 2.8 collective-permute-done.3
  220.4 4.9 %fusion.7 = bf16[8,2,256,512]{3,2,1,0:T(8,128)(2,1)} fusion(bf16[8,2,128,512]{3,2,1,0:T(8,128)(2,1)S(1)} %collective-permute-done.3, bf16[8,2,128,512]{3,2,1,0:T(8,128)(2,1)} %get-tuple-element.7, pred[8,2,128,256]{2,3,1,0:T(32,128)(4,1)S(1)} %iota_compare_fusion, pred[8,2,128,256]{2,3,1,0:T(32,128)(4,1)S(1)} %iota_compare_fusion.1), kind=kOutput, calls=%fused_computation.13 | convolution fusion | flops 1085276160 | bytes 9437184 | tf_op jit(solution)/shard_map/spct,spcl->sptl/dot_general | solution.py:170
  225.6 1.9 dynamic_slice.19
  227.5 84.3 %reduce-scatter.2.cloned.1.call-done = bf16[512,512]{1,0:T(8,128)(2,1)} async-done(((bf16[4096,512]{1,0:T(8,128)(2,1)}), bf16[512,512]{1,0:T(8,128)(2,1)}) %reduce-scatter.2.cloned.1.call-update) | async-done | bytes 524304 | tf_op jit(solution)/shard_map/reduce_scatter | solution.py:173
  311.7 1.1 fusion.31
  312.9 7.9 %reshape.139 = bf16[512,4,2,512]{3,2,1,0:T(2,128)(2,1)} reshape(bf16[512,4096]{1,0:T(8,128)(2,1)} %constant_dynamic-update-slice_fusion) | data formatting | bytes 8388608 | tf_op jit(solution)/shard_map/reshape | solution.py:178
  320.8 14.3 %dynamic-slice_reduce_fusion = bf16[512,4,512]{2,1,0:T(4,128)(2,1)S(1)} fusion(bf16[512,4,2,512]{3,2,1,0:T(2,128)(2,1)} %reshape.139, s32[]{:T(128)S(6)} %select_n.104), kind=kLoop, calls=%fused_computation.9 | loop fusion | bytes 4194308 | tf_op jit(solution)/shard_map/jit(dynamic_index_in_dim)/dynamic_slice | solution.py:179
  336.4 50.8 %all-gather.11.cloned.1.call-done = bf16[4096,512]{1,0:T(8,128)(2,1)} async-done(((bf16[512,512]{1,0:T(8,128)(2,1)}), bf16[4096,512]{1,0:T(8,128)(2,1)}) %all-gather.11.cloned.1.call-update) | async-done | bytes 4194320 | tf_op jit(solution)/shard_map/all_gather | solution.py:26
  387.1 2.2 copy-done.4
  389.3 4.7 %shard_map.83 = bf16[512,2048]{1,0:T(8,128)(2,1)S(1)} custom-call(bf16[512,1024]{1,0:T(8,128)(2,1)S(1)} %pad_maximum_fusion.2.a_ref, bf16[8,512,512]{2,1,0:T(8,128)(2,1)S(1)} %bitcast.66, bf16[512,2048]{1,0:T(8,128)(2,1)S(1)} %bitcast.64), custom_call_target="tpu_custom_call" | custom-call | tf_op jit(solution)/shard_map/pallas_call | solution.py:80
  394.2 1.6 squeeze.24
  395.8 0.8 squeeze.23
  396.6 2.1 collective-permute-done.5
  398.8 1.5 pad_maximum_fusion.1
  400.3 4.6 %copy.51 = bf16[256,4,2,512]{3,2,1,0:T(2,128)(2,1)} copy(bf16[256,4,2,512]{3,1,0,2:T(4,128)(2,1)S(1)} %pad_maximum_fusion.1) | data formatting | bytes 4194304 | tf_op jit(solution)/shard_map/concatenate | solution.py:18
  404.9 4.5 %reshape.141 = bf16[256,4096]{1,0:T(8,128)(2,1)} reshape(bf16[256,4,2,512]{3,2,1,0:T(2,128)(2,1)} %copy.51) | data formatting | bytes 4194304 | tf_op jit(solution)/shard_map/reshape | solution.py:182
  (68 shorter events, 4.4 us)
Async XLA Ops:
  6.5 191.0 %copy-start = (bf16[1,768,1024]{2,1,0:T(8,128)(2,1)S(1)}, bf16[1,768,1024]{2,1,0:T(8,128)(2,1)}, u32[]{:S(2)}) copy-start(bf16[1,768,1024]{2,1,0:T(8,128)(2,1)} %param.15) | copy-start | bytes 4718596
  6.5 79.0 %all-gather.7.cloned.1.call-start = ((), (), s32[]{:S(2)}) async-start(), calls=%async_computation.2 | async-start | bytes 4718592 | tf_op jit(solution)/shard_map/all_gather | solution.py:26
  8.6 159.4 %all-gather.9.cloned.1.call-start = ((), (), s32[]{:S(2)}) async-start(), calls=%async_computation.3 | async-start | bytes 4866048 | tf_op jit(solution)/shard_map/all_gather | solution.py:122
  8.7 12.6 %collective-permute-start = (bf16[256,4096]{1,0:T(8,128)(2,1)}, bf16[256,4096]{1,0:T(8,128)(2,1)}, u32[]{:S(2)}, u32[]{:S(2)}) collective-permute-start(bf16[256,4096]{1,0:T(8,128)(2,1)} %param.8), channel_id=1, source_target_pairs={{0,4},{4,0},{1,5},{5,1},{2,6},{6,2},{3,7},{7,3},{8,12},{12,8},{9,1... | collective-permute-start | bytes 6291464 | tf_op jit(solution)/shard_map/ppermute | solution.py:13
  9.9 11.3 %collective-permute-start.1 = (s32[8,256]{1,0:T(8,128)S(1)}, s32[8,256]{1,0:T(8,128)S(1)}, u32[]{:S(2)}, u32[]{:S(2)}) collective-permute-start(s32[8,256]{1,0:T(8,128)S(1)} %get-tuple-element.24), channel_id=1, source_target_pairs={{0,4},{4,0},{1,5},{5,1},{2,6},{6,2},{3,7},{7,3},{8,12},{12,8},{9,1... | collective-permute-start | bytes 24584 | tf_op jit(solution)/shard_map/ppermute | solution.py:13
  31.2 3.3 copy-start.5
  85.6 2.2 copy-start.2
  87.8 2.2 copy-start.3
  94.5 217.2 %reduce-scatter.2.cloned.1.call-start = ((), (), s32[]{:S(2)}) async-start(), calls=%async_computation.1 | async-start | bytes 4718592 | tf_op jit(solution)/shard_map/reduce_scatter | solution.py:173
  182.5 4.5 %collective-permute-start.2 = (bf16[8,2,128,512]{3,2,1,0:T(8,128)(2,1)}, bf16[8,2,128,512]{3,2,1,0:T(8,128)(2,1)}, u32[]{:S(2)}, u32[]{:S(2)}) collective-permute-start(bf16[8,2,128,512]{3,2,1,0:T(8,128)(2,1)} %rev.6), channel_id=1, source_target_pairs={{0,4},{4,0},{1,5},{5,1},{2,6},{6,2},{3,7},{7,3},{8,12},{12,8},{9,1... | collective-permute-start | bytes 6291464 | tf_op jit(solution)/shard_map/ppermute | solution.py:13
  190.8 1.4 copy-start.8
  191.4 6.1 %copy-start.6 = (bf16[8,2,128,1024]{3,2,1,0:T(8,128)(2,1)}, bf16[8,2,128,1024]{3,2,1,0:T(8,128)(2,1)S(1)}, u32[]{:S(2)}) copy-start(bf16[8,2,128,1024]{3,2,1,0:T(8,128)(2,1)S(1)} %pad_maximum_fusion) | copy-start | bytes 12582916
  216.0 4.4 %collective-permute-start.3 = (bf16[8,2,128,512]{3,2,1,0:T(8,128)(2,1)}, bf16[8,2,128,512]{3,2,1,0:T(8,128)(2,1)S(1)}, u32[]{:S(2)}, u32[]{:S(2)}) collective-permute-start(bf16[8,2,128,512]{3,2,1,0:T(8,128)(2,1)} %rev.7), channel_id=1, source_target_pairs={{0,4},{4,0},{1,5},{5,1},{2,6},{6,2},{3,7},{7,3},{8,12},{12,8},{9,1... | collective-permute-start | bytes 6291464 | tf_op jit(solution)/shard_map/ppermute | solution.py:13
  225.3 161.8 %all-gather.11.cloned.1.call-start = ((), (), s32[]{:S(2)}) async-start(), calls=%async_computation.4 | async-start | bytes 4718592 | tf_op jit(solution)/shard_map/all_gather | solution.py:26
  312.8 22.9 %collective-permute-start.4 = (bf16[512,512]{1,0:T(8,128)(2,1)S(1)}, bf16[512,512]{1,0:T(8,128)(2,1)S(1)}, u32[]{:S(2)}, u32[]{:S(2)}) collective-permute-start(bf16[512,512]{1,0:T(8,128)(2,1)S(1)} %pad_maximum_fusion.4), channel_id=1, source_target_pairs={{0,4},{4,0},{1,5},{5,1},{2,6},{6,2},{3,7},{7,3},{8,12},{12,8},{9,1... | collective-permute-start | bytes 1572872 | tf_op jit(solution)/shard_map/ppermute | solution.py:13
  335.1 1.0 copy-start.7
  387.1 2.2 copy-start.4
  395.8 2.9 collective-permute-start.5
  400.3 9.0 %copy-start.1 = (bf16[1,768,1024]{2,1,0:T(8,128)(2,1)S(1)}, bf16[1,768,1024]{2,1,0:T(8,128)(2,1)}, u32[]{:S(2)}) copy-start(bf16[1,768,1024]{2,1,0:T(8,128)(2,1)} %param.15) | copy-start | bytes 4718596
Sparse Core Ops, SparseCore 0:
  9.5 76.0 all-gather.6
  94.6 73.2 all-gather.8
  225.4 86.2 reduce-scatter.1
  313.9 73.1 all-gather.10

commit v4 on v2

--- a/solution.py
+++ b/solution.py
@@ -12,6 +12,26 @@
     part = w.shape[0] // lax.axis_size("node")
     piece = lax.dynamic_slice_in_dim(w, lax.axis_index("node") * part, part, axis=0)
     return lax.all_gather(piece, GROUP, axis=0)
+
+
+def gather_up(w):
+    n_node, n_local = lax.axis_size("node"), lax.axis_size("local")
+    here, core = lax.axis_index("local"), lax.axis_index("node") % 2
+    half, columns = w.shape[0] // 2, w.shape[1]
+    pair = [(i, i ^ 1) for i in range(n_node)]
+    mine = lax.dynamic_slice_in_dim(w, core * half, half, axis=0)
+    whole = jnp.zeros((n_local, 2, half, columns), w.dtype)
+    whole = lax.dynamic_update_slice(whole, w.reshape(1, 2, half, columns), (here, 0, 0, 0))
+    for way, steps in ((1, n_local // 2), (-1, (n_local - 1) // 2)):
+        ring = [(i, (i + way) % n_local) for i in range(n_local)]
+        block = mine
+        for step in range(1, steps + 1):
+            block = lax.ppermute(block, "local", ring)
+            other = lax.ppermute(block, "node", pair)
+            source = (here - way * step) % n_local
+            whole = lax.dynamic_update_slice(whole, block[None, None], (source, core, 0, 0))
+            whole = lax.dynamic_update_slice(whole, other[None, None], (source, 1 - core, 0, 0))
+    return whole.reshape(n_local * 2, half, columns)
 
 
 def down_kernel(a_ref, w_ref, out_ref, total):
@@ -62,16 +82,16 @@
 
 
 def up_project(a, pieces, tokens):
-    n_node, n_local = lax.axis_size("node"), lax.axis_size("local")
+    n_local = lax.axis_size("local")
     _, part, columns = pieces.shape
     rows = a.shape[0]
     return pl.pallas_call(
         up_kernel,
-        grid=(n_local, n_node),
+        grid=(n_local, 2),
         out_shape=jax.ShapeDtypeStruct(tokens.shape, jnp.bfloat16),
         in_specs=[
             pl.BlockSpec((rows, part), lambda c, k: (0, k)),
-            pl.BlockSpec((1, part, columns), lambda c, k: (k * n_local + c, 0, 0)),
+            pl.BlockSpec((1, part, columns), lambda c, k: (c * 2 + k, 0, 0)),
             pl.BlockSpec((rows, columns), lambda c, k: (0, c)),
         ],
         out_specs=pl.BlockSpec((rows, columns), lambda c, k: (0, c)),
@@ -138,7 +158,7 @@
     total = total.astype(jnp.bfloat16).reshape(owners * tok_rows, width)
     combined = lax.psum_scatter(total, GROUP, scatter_dimension=0, tiled=True)
 
-    return up_project(combined, gather_weight(w_up), tokens)
+    return up_project(combined, gather_up(w_up), tokens)
 
 
 def solution(mesh):

time: 377 us -> 372 us (0.987)
  waiting for transfers between devices: 288 us -> 267 us
  local copies, waits for them, and re-layouts: 20.7 us -> 33.6 us
  starting transfers between devices: 0.31 us -> 4.69 us
    ppermute x0 -> x6, waiting for transfers between devices: none -> 102 us  [the longest x3 102 us: gather_up(): block = lax.ppermute(block, 'local', ring)]
    reduce_scatter x1, waiting for transfers between devices: 107 us -> 22.5 us  [local(): combined = lax.psum_scatter(total, GROUP, scatter_dimension=0, tiled=True)]
    all_gather x2 -> x1, waiting for transfers between devices: 107 us -> 65.5 us  [gather_weight(): return lax.all_gather(piece, GROUP, axis=0)]
    dynamic_update_slice x0 -> x7, local copies, waits for them, and re-layouts: none -> 7.07 us  [the longest x3 4 us: gather_up(): lax.dynamic_update_slice(whole, block[None, None], (source, core, 0, 0))]
    unnamed x22 -> x24, local copies, waits for them, and re-layouts: 11.5 us -> 16.2 us
    ppermute x0 -> x6, starting transfers between devices: none -> 4.6 us  [the longest x3 4.6 us: gather_up(): block = lax.ppermute(block, 'local', ring)]
  transfers between devices with their start and end apart: 4 -> 9, of which waited for: 4 -> 6; matrix products, arithmetic and copies ran while one was open for 13% -> 6% of each run, Pallas kernels for 0% -> 0%
where the time goes in v4:
time: 372 us; the launch traced here: 371 us
  waiting for transfers between devices  267 us (72%)
  local copies, waits for them, and re-layouts  33.6 us (9%)
  matrix products  33 us (9%)
  between operations  13.4 us (4%)
  Pallas kernels  11 us (3%)
  other arithmetic  8.66 us (2%)
  starting transfers between devices  4.69 us (1%)
    ppermute x3, waiting for transfers between devices, gather_up(): block = lax.ppermute(block, 'local', ring)  102 us
    all_gather x1, waiting for transfers between devices, local(): everyone = lax.all_gather(jnp.concatenate([latent, coded]), GROUP, axis=0)  76.5 us
    all_gather x1, waiting for transfers between devices, gather_weight(): return lax.all_gather(piece, GROUP, axis=0)  65.5 us
    reduce_scatter x1, waiting for transfers between devices, local(): combined = lax.psum_scatter(total, GROUP, scatter_dimension=0, tiled=True)  22.5 us
    unnamed x24, local copies, waits for them, and re-layouts  16.2 us
    dot_general x1, matrix products, local(): answer = jnp.dot(hidden, expert_down[j], preferred_element_type=jnp.float32)  13.5 us
  transfers between devices with their start and end apart: 9, of which 6 were waited for; matrix products, arithmetic and copies ran while one was open for 6% of the time, Pallas kernels for 0%

profile of v4, /device:TPU:0, one launch (start us, length us, event | category | flops | bytes accessed | tf_op | source)
XLA Modules:
  0.0 371.2 jit_solution(10857766604322177385)
XLA Ops:
  6.5 1.6 copy-done
  8.1 0.8 constant_dynamic-slice_fusion.1
  9.0 0.0 all-gather.7.cloned.1.call-start
  9.0 0.8 convert_bitcast_fusion.1
  9.9 0.7 fusion.16
  10.6 2.1 fusion
  12.8 1.9 fusion.1
  14.7 4.5 %reshape.84 = bf16[256,4,4,256]{3,2,1,0:T(4,128)(2,1)} reshape(bf16[256,4096]{1,0:T(8,128)(2,1)} %fusion.1) | data formatting | bytes 4194304 | tf_op jit(solution)/shard_map/reshape | solution.py:54
  19.2 2.5 copy.10
  21.7 65.5 %all-gather.5.cloned.1.call-done = bf16[4096,1024]{1,0:T(8,128)(2,1)} async-done(((bf16[256,1024]{1,0:T(8,128)(2,1)}), bf16[4096,1024]{1,0:T(8,128)(2,1)}) %all-gather.5.cloned.1.call-update) | async-done | bytes 8388624 | tf_op jit(solution)/shard_map/all_gather | solution.py:14
  87.2 3.4 copy-done.6
  90.6 5.1 %shard_map.82 = bf16[256,1024]{1,0:T(8,128)(2,1)S(1)} custom-call(bf16[16,256,256]{2,1,0:T(8,128)(2,1)S(1)} %bitcast.86, bf16[16,256,1024]{2,1,0:T(8,128)(2,1)S(1)} %bitcast.85), custom_call_target="tpu_custom_call" | custom-call | tf_op jit(solution)/shard_map/pallas_call | solution.py:56
  95.7 0.8 pad_maximum_fusion
  96.6 76.5 %all-gather.7.cloned.1.call-done = bf16[4352,1024]{1,0:T(8,128)(2,1)} async-done(((bf16[272,1024]{1,0:T(8,128)(2,1)}), bf16[4352,1024]{1,0:T(8,128)(2,1)}) %all-gather.7.cloned.1.call-update) | async-done | bytes 8912912 | tf_op jit(solution)/shard_map/all_gather | solution.py:123
  173.2 1.1 slice.28
  174.2 0.3 copy.16
  174.6 0.1 reshape.97
  174.7 0.1 fusion.18
  174.7 0.1 fusion.10
  174.8 0.6 reduce-window.6
  175.4 0.2 slice_reduce_fusion
  175.7 0.1 bitcast_select_fusion
  175.7 1.4 select_reduce_fusion
  177.2 7.4 %convolution_convert_fusion.1 = bf16[16,128,1024]{2,1,0:T(8,128)(2,1)S(1)} fusion(bf16[16,272,1024]{2,1,0:T(8,128)(2,1)} %bitcast.89, s32[16,272]{1,0:T(8,128)S(1)} %pad.9), kind=kOutput, calls=%fused_computation.7 | convolution fusion | flops 1143504896 | bytes 13124608 | tf_op jit(solution)/shard_map/sct,stl->scl/dot_general | solution.py:142
  184.6 5.3 %fusion.5 = f32[2048,768]{1,0:T(8,128)} fusion(bf16[2048,1024]{1,0:T(8,128)(2,1)S(1)} %bitcast.91, bf16[1,1024,768]{2,1,0:T(8,128)(2,1)S(1)} %copy-done.10), kind=kOutput, calls=%fused_computation.13 | convolution fusion | flops 3221225472 | bytes 12058624 | tf_op jit(solution)/shard_map/dot_general | solution.py:146
  189.9 13.5 %multiply_convert_fusion = bf16[2048,1024]{1,0:T(8,128)(2,1)} fusion(f32[2048]{0:T(1024)S(1)} %bitcast.97, f32[2048,768]{1,0:T(8,128)} %fusion.5, bf16[2048,1024]{1,0:T(8,128)(2,1)} %bitcast.92, bf16[1,768,1024]{2,1,0:T(8,128)(2,1)} %param.15, bf16[1,1024,768]{2,1,0:T(8,128)(2,1)} %param.14), kind=kOutput, calls=%fused_computation | convolution fusion | flops 6456082432 | bytes 17833984 | tf_op jit(solution)/shard_map/dot_general | solution.py:149
  203.4 6.9 %convolution_convert_fusion = bf16[16,256,1024]{2,1,0:T(8,128)(2,1)} fusion(bf16[16,128,1024]{2,1,0:T(8,128)(2,1)} %bitcast.90, s32[16,256]{1,0:T(8,128)S(1)} %bitcast_select_fusion), kind=kOutput, calls=%fused_computation.1 | convolution fusion | flops 1078460416 | bytes 12599296 | tf_op jit(solution)/shard_map/sct,scl->stl/dot_general | solution.py:151
  210.3 1.5 copy-done.9
  211.8 0.1 constant_dynamic-slice_fusion
  211.9 0.8 collective-permute-start
  212.7 26.5 %collective-permute-done = bf16[512,1024]{1,0:T(8,128)(2,1)} collective-permute-done((bf16[512,1024]{1,0:T(8,128)(2,1)S(1)}, bf16[512,1024]{1,0:T(8,128)(2,1)}, u32[]{:S(2)}, u32[]{:S(2)}) %collective-permute-start) | collective-permute-done | bytes 1048608 | tf_op jit(solution)/shard_map/ppermute | solution.py:29
  239.2 3.8 %collective-permute-start.4 = (bf16[512,1024]{1,0:T(8,128)(2,1)S(1)}, bf16[512,1024]{1,0:T(8,128)(2,1)}, u32[]{:S(2)}, u32[]{:S(2)}) collective-permute-start(bf16[512,1024]{1,0:T(8,128)(2,1)S(1)} %constant_dynamic-slice_fusion), channel_id=1, source_target_pairs={{0,3},{1,0},{2,1},{3,2},{4,7},{5,4},{6,5},{7,6},{8,11},{9,8},{10,9... | collective-permute-start | bytes 3145736 | tf_op jit(solution)/shard_map/ppermute | solution.py:29
  243.0 46.2 %collective-permute-done.2 = bf16[512,1024]{1,0:T(8,128)(2,1)} collective-permute-done((bf16[512,1024]{1,0:T(8,128)(2,1)}, bf16[512,1024]{1,0:T(8,128)(2,1)}, u32[]{:S(2)}, u32[]{:S(2)}) %collective-permute-start.2) | collective-permute-done | bytes 1048608 | tf_op jit(solution)/shard_map/ppermute | solution.py:29
  289.2 1.1 broadcast_in_dim.48
  290.3 0.3 constant_dynamic-update-slice_fusion
  290.6 29.4 %collective-permute-done.4 = bf16[512,1024]{1,0:T(8,128)(2,1)} collective-permute-done((bf16[512,1024]{1,0:T(8,128)(2,1)S(1)}, bf16[512,1024]{1,0:T(8,128)(2,1)}, u32[]{:S(2)}, u32[]{:S(2)}) %collective-permute-start.4) | collective-permute-done | bytes 1048608 | tf_op jit(solution)/shard_map/ppermute | solution.py:29
  320.0 1.3 bitcast_dynamic-update-slice_fusion.5
  321.3 1.3 bitcast_dynamic-update-slice_fusion.4
  322.7 1.3 bitcast_dynamic-update-slice_fusion.3
  324.0 1.4 bitcast_dynamic-update-slice_fusion.2
  325.4 1.3 bitcast_dynamic-update-slice_fusion.1
  326.7 0.1 bitcast_dynamic-update-slice_fusion
  326.9 3.2 copy-done.2
  330.1 22.5 %reduce-scatter.2.cloned.1.call-done.a_ref = bf16[256,1024]{1,0:T(8,128)(2,1)} async-done(((bf16[4096,1024]{1,0:T(8,128)(2,1)}), bf16[256,1024]{1,0:T(8,128)(2,1)}) %reduce-scatter.2.cloned.1.call-update) | async-done | bytes 524304 | tf_op jit(solution)/shard_map/reduce_scatter | solution.py:159
  352.6 3.5 copy-done.3
  356.1 1.6 copy-done.5
  357.7 1.0 copy-done.7
  358.7 5.9 %shard_map.83 = bf16[256,4096]{1,0:T(8,128)(2,1)} custom-call(bf16[256,1024]{1,0:T(8,128)(2,1)S(1)} %copy-done.7, bf16[8,512,1024]{2,1,0:T(8,128)(2,1)S(1)} %bitcast.84, bf16[256,4096]{1,0:T(8,128)(2,1)S(1)} %copy-done.5), custom_call_target="tpu_custom_call" | custom-call | tf_op jit(solution)/shard_map/pallas_call | solution.py:88
  (38 shorter events, 0.3 us)
Async XLA Ops:
  6.5 1.6 copy-start
  6.5 80.7 %all-gather.5.cloned.1.call-start = ((), (), s32[]{:S(2)}) async-start(), calls=%async_computation.2 | async-start | bytes 8912896 | tf_op jit(solution)/shard_map/all_gather | solution.py:14
  9.0 3.8 %copy-start.4 = (bf16[256,4096]{1,0:T(8,128)(2,1)S(1)}, bf16[256,4096]{1,0:T(8,128)(2,1)}, u32[]{:S(2)}) copy-start(bf16[256,4096]{1,0:T(8,128)(2,1)} %tok_ref.1) | copy-start | bytes 6291460
  9.0 164.2 %all-gather.7.cloned.1.call-start = ((), (), s32[]{:S(2)}) async-start(), calls=%async_computation.3 | async-start | bytes 9469952 | tf_op jit(solution)/shard_map/all_gather | solution.py:123
  87.2 3.4 copy-start.6
  96.5 256.0 %reduce-scatter.2.cloned.1.call-start = ((), (), s32[]{:S(2)}) async-start(), calls=%async_computation.1 | async-start | bytes 8912896 | tf_op jit(solution)/shard_map/reduce_scatter | solution.py:159
  177.2 7.4 %copy-start.10 = (bf16[1,1024,768]{2,1,0:T(8,128)(2,1)S(1)}, bf16[1,1024,768]{2,1,0:T(8,128)(2,1)}, u32[]{:S(2)}) copy-start(bf16[1,1024,768]{2,1,0:T(8,128)(2,1)} %param.13) | copy-start | bytes 4718596
  184.6 5.3 %copy-start.8 = (bf16[16,128,1024]{2,1,0:T(8,128)(2,1)}, bf16[16,128,1024]{2,1,0:T(8,128)(2,1)S(1)}, u32[]{:S(2)}) copy-start(bf16[16,128,1024]{2,1,0:T(8,128)(2,1)S(1)} %convolution_convert_fusion.1) | copy-start | bytes 12582916
  210.2 1.6 copy-start.9
  211.9 27.3 %collective-permute-start = (bf16[512,1024]{1,0:T(8,128)(2,1)S(1)}, bf16[512,1024]{1,0:T(8,128)(2,1)}, u32[]{:S(2)}, u32[]{:S(2)}) collective-permute-start(bf16[512,1024]{1,0:T(8,128)(2,1)S(1)} %constant_dynamic-slice_fusion), channel_id=1, source_target_pairs={{0,1},{1,2},{2,3},{3,0},{4,5},{5,6},{6,7},{7,4},{8,9},{9,10},{10,1... | collective-permute-start | bytes 3145736 | tf_op jit(solution)/shard_map/ppermute | solution.py:29
  239.2 50.0 %collective-permute-start.2 = (bf16[512,1024]{1,0:T(8,128)(2,1)}, bf16[512,1024]{1,0:T(8,128)(2,1)}, u32[]{:S(2)}, u32[]{:S(2)}) collective-permute-start(bf16[512,1024]{1,0:T(8,128)(2,1)} %collective-permute-done), channel_id=1, source_target_pairs={{0,1},{1,2},{2,3},{3,0},{4,5},{5,6},{6,7},{7,4},{8,9},{9,10},{10,1... | collective-permute-start | bytes 3145736 | tf_op jit(solution)/shard_map/ppermute | solution.py:29
  239.2 80.8 %collective-permute-start.4 = (bf16[512,1024]{1,0:T(8,128)(2,1)S(1)}, bf16[512,1024]{1,0:T(8,128)(2,1)}, u32[]{:S(2)}, u32[]{:S(2)}) collective-permute-start(bf16[512,1024]{1,0:T(8,128)(2,1)S(1)} %constant_dynamic-slice_fusion), channel_id=1, source_target_pairs={{0,3},{1,0},{2,1},{3,2},{4,7},{5,4},{6,5},{7,6},{8,11},{9,8},{10,9... | collective-permute-start | bytes 3145736 | tf_op jit(solution)/shard_map/ppermute | solution.py:29
  243.0 78.3 %collective-permute-start.1 = (bf16[512,1024]{1,0:T(8,128)(2,1)}, bf16[512,1024]{1,0:T(8,128)(2,1)}, u32[]{:S(2)}, u32[]{:S(2)}) collective-permute-start(bf16[512,1024]{1,0:T(8,128)(2,1)} %collective-permute-done), channel_id=1, source_target_pairs={{0,4},{4,0},{8,12},{12,8},{1,5},{5,1},{9,13},{13,9},{2,6},{6,2},{1... | collective-permute-start | bytes 3145736 | tf_op jit(solution)/shard_map/ppermute | solution.py:30
  289.2 34.8 %collective-permute-start.3 = (bf16[512,1024]{1,0:T(8,128)(2,1)}, bf16[512,1024]{1,0:T(8,128)(2,1)}, u32[]{:S(2)}, u32[]{:S(2)}) collective-permute-start(bf16[512,1024]{1,0:T(8,128)(2,1)} %collective-permute-done.2), channel_id=1, source_target_pairs={{0,4},{4,0},{8,12},{12,8},{1,5},{5,1},{9,13},{13,9},{2,6},{6,2},{1... | collective-permute-start | bytes 3145736 | tf_op jit(solution)/shard_map/ppermute | solution.py:30
  320.0 6.8 %collective-permute-start.5 = (bf16[512,1024]{1,0:T(8,128)(2,1)}, bf16[512,1024]{1,0:T(8,128)(2,1)S(1)}, u32[]{:S(2)}, u32[]{:S(2)}) collective-permute-start(bf16[512,1024]{1,0:T(8,128)(2,1)} %collective-permute-done.4), channel_id=1, source_target_pairs={{0,4},{4,0},{8,12},{12,8},{1,5},{5,1},{9,13},{13,9},{2,6},{6,2},{1... | collective-permute-start | bytes 3145736 | tf_op jit(solution)/shard_map/ppermute | solution.py:30
  326.9 3.2 copy-start.2
  352.6 12.1 %copy-start.1 = (bf16[1024,1024]{1,0:T(8,128)(2,1)S(1)}, bf16[1024,1024]{1,0:T(8,128)(2,1)}, u32[]{:S(2)}) copy-start(bf16[1024,1024]{1,0:T(8,128)(2,1)} %param.11) | copy-start | bytes 6291460
  352.6 3.5 copy-start.3
  356.1 1.6 copy-start.5
  357.7 1.0 copy-start.7
Sparse Core Ops, SparseCore 0:
  9.6 77.5 all-gather.4
  96.7 76.4 all-gather.6
  210.4 142.1 reduce-scatter.1

commit v5 on v4

--- a/solution.py
+++ b/solution.py
@@ -120,6 +120,7 @@
         jnp.bfloat16
     )
     latent = down_project(normed, gather_weight(w_down))
+    up = gather_up(w_up)
     everyone = lax.all_gather(jnp.concatenate([latent, coded]), GROUP, axis=0)
     codes = everyone[:, tok_rows:].reshape(owners, -1)[:, : 3 * top_k * tok_rows]
     codes = codes.astype(jnp.int32).reshape(owners, 3, top_k, tok_rows)
@@ -142,7 +143,7 @@
         rows = jnp.einsum(
             "sct,stl->scl", longer.astype(jnp.bfloat16), everyone, preferred_element_type=jnp.float32
         ).astype(jnp.bfloat16)
-        rows = rows.reshape(owners * capacity, width)
+        rows, up = lax.optimization_barrier((rows.reshape(owners * capacity, width), up))
         gate = jnp.dot(rows, expert_gate[j], preferred_element_type=jnp.float32)
         upper = jnp.dot(rows, expert_up[j], preferred_element_type=jnp.float32)
         hidden = (jax.nn.silu(gate) * upper).astype(jnp.bfloat16)
@@ -158,7 +159,7 @@
     total = total.astype(jnp.bfloat16).reshape(owners * tok_rows, width)
     combined = lax.psum_scatter(total, GROUP, scatter_dimension=0, tiled=True)
 
-    return up_project(combined, gather_up(w_up), tokens)
+    return up_project(combined, up, tokens)
 
 
 def solution(mesh):

time: 372 us -> 396 us (1.065)
  waiting for transfers between devices: 267 us -> 294 us
    reduce_scatter x1, waiting for transfers between devices: 22.5 us -> 105 us  [local(): combined = lax.psum_scatter(total, GROUP, scatter_dimension=0, tiled=True)]
    all_gather x1, waiting for transfers between devices: 76.5 us -> 0.01 us  [local(): everyone = lax.all_gather(jnp.concatenate([latent, coded]), GROUP, axis=0)]
    ppermute x3, waiting for transfers between devices: 102 us -> 120 us  [gather_up(): block = lax.ppermute(block, 'local', ring)]
    unnamed x24 -> x26, local copies, waits for them, and re-layouts: 16.2 us -> 15.1 us
  transfers between devices with their start and end apart: 9 -> 9, of which waited for: 6 -> 5; matrix products, arithmetic and copies ran while one was open for 6% -> 5% of each run, Pallas kernels for 0% -> 0%
where the time goes in v5:
time: 396 us; the launch traced here: 395 us
  waiting for transfers between devices  294 us (74%)
  matrix products  33 us (8%)
  local copies, waits for them, and re-layouts  31.8 us (8%)
  between operations  13.4 us (3%)
  Pallas kernels  11 us (3%)
  other arithmetic  7.43 us (2%)
  starting transfers between devices  4.86 us (1%)
    ppermute x3, waiting for transfers between devices, gather_up(): block = lax.ppermute(block, 'local', ring)  120 us
    reduce_scatter x1, waiting for transfers between devices, local(): combined = lax.psum_scatter(total, GROUP, scatter_dimension=0, tiled=True)  105 us
    all_gather x1, waiting for transfers between devices, gather_weight(): return lax.all_gather(piece, GROUP, axis=0)  68.6 us
    unnamed x26, local copies, waits for them, and re-layouts  15.1 us
    dot_general x1, matrix products, local(): answer = jnp.dot(hidden, expert_down[j], preferred_element_type=jnp.float32)  13.5 us
  transfers between devices with their start and end apart: 9, of which 5 were waited for; matrix products, arithmetic and copies ran while one was open for 5% of the time, Pallas kernels for 0%

profile of v5, /device:TPU:0, one launch (start us, length us, event | category | flops | bytes accessed | tf_op | source)
XLA Modules:
  0.0 395.3 jit_solution(2662904160744854829)
XLA Ops:
  6.5 1.6 copy-done
  8.1 0.9 constant_dynamic-slice_fusion.1
  9.0 0.0 all-gather.5.cloned.1.call-update
  9.0 0.0 all-gather.7.cloned.1.call-start
  9.1 2.1 fusion
  11.2 2.2 fusion.1
  13.4 2.8 reshape.84
  16.1 2.3 copy.10
  18.6 68.6 %all-gather.5.cloned.1.call-done = bf16[4096,1024]{1,0:T(8,128)(2,1)} async-done(((bf16[256,1024]{1,0:T(8,128)(2,1)}), bf16[4096,1024]{1,0:T(8,128)(2,1)}) %all-gather.5.cloned.1.call-update) | async-done | bytes 8388624 | tf_op jit(solution)/shard_map/all_gather | solution.py:14
  87.2 3.4 copy-done.5
  90.6 5.1 %shard_map.82 = bf16[256,1024]{1,0:T(8,128)(2,1)S(1)} custom-call(bf16[16,256,256]{2,1,0:T(8,128)(2,1)S(1)} %bitcast.86, bf16[16,256,1024]{2,1,0:T(8,128)(2,1)S(1)} %bitcast.85), custom_call_target="tpu_custom_call" | custom-call | tf_op jit(solution)/shard_map/pallas_call | solution.py:56
  95.7 0.8 pad_maximum_fusion
  96.5 0.0 all-gather.7.cloned.1.call-update
  96.5 0.0 reduce-scatter.2.cloned.1.call-start
  96.6 1.3 constant_dynamic-slice_fusion
  97.9 0.9 collective-permute-start
  98.9 44.1 %collective-permute-done = bf16[512,1024]{1,0:T(8,128)(2,1)} collective-permute-done((bf16[512,1024]{1,0:T(8,128)(2,1)S(1)}, bf16[512,1024]{1,0:T(8,128)(2,1)}, u32[]{:S(2)}, u32[]{:S(2)}) %collective-permute-start) | collective-permute-done | bytes 1048608 | tf_op jit(solution)/shard_map/ppermute | solution.py:29
  143.0 3.8 collective-permute-start.4
  146.8 45.4 %collective-permute-done.2 = bf16[512,1024]{1,0:T(8,128)(2,1)} collective-permute-done((bf16[512,1024]{1,0:T(8,128)(2,1)}, bf16[512,1024]{1,0:T(8,128)(2,1)}, u32[]{:S(2)}, u32[]{:S(2)}) %collective-permute-start.2) | collective-permute-done | bytes 1048608 | tf_op jit(solution)/shard_map/ppermute | solution.py:29
  192.2 1.1 broadcast_in_dim.45
  193.3 0.5 copy-done.8
  193.8 0.3 constant_dynamic-update-slice_fusion
  194.1 30.5 %collective-permute-done.4 = bf16[512,1024]{1,0:T(8,128)(2,1)} collective-permute-done((bf16[512,1024]{1,0:T(8,128)(2,1)S(1)}, bf16[512,1024]{1,0:T(8,128)(2,1)}, u32[]{:S(2)}, u32[]{:S(2)}) %collective-permute-start.4) | collective-permute-done | bytes 1048608 | tf_op jit(solution)/shard_map/ppermute | solution.py:29
  224.6 1.3 bitcast_dynamic-update-slice_fusion.5
  225.9 1.3 bitcast_dynamic-update-slice_fusion.4
  227.3 1.3 bitcast_dynamic-update-slice_fusion.3
  228.6 1.3 bitcast_dynamic-update-slice_fusion.2
  230.0 1.3 bitcast_dynamic-update-slice_fusion.1
  231.3 0.1 bitcast_dynamic-update-slice_fusion
  231.5 3.2 copy-done.2
  234.7 1.1 slice.28
  235.8 0.3 copy.16
  236.1 0.1 reshape.97
  236.2 0.1 fusion.18
  236.3 0.6 reduce-window.6
  236.9 0.2 slice_reduce_fusion
  237.1 0.1 bitcast_select_fusion
  237.2 7.4 %convolution_convert_fusion.1 = bf16[16,128,1024]{2,1,0:T(8,128)(2,1)S(1)} fusion(bf16[16,272,1024]{2,1,0:T(8,128)(2,1)} %bitcast.89, s32[16,272]{1,0:T(8,128)S(1)} %pad.9), kind=kOutput, calls=%fused_computation.7 | convolution fusion | flops 1143504896 | bytes 13124608 | tf_op jit(solution)/shard_map/sct,stl->scl/dot_general | solution.py:143
  244.6 0.1 fusion.10
  244.7 1.4 select_reduce_fusion
  246.1 5.3 %fusion.5 = f32[2048,768]{1,0:T(8,128)} fusion(bf16[2048,1024]{1,0:T(8,128)(2,1)S(1)} %bitcast.91, bf16[1,1024,768]{2,1,0:T(8,128)(2,1)S(1)} %copy-done.11), kind=kOutput, calls=%fused_computation.13 | convolution fusion | flops 3221225472 | bytes 12058624 | tf_op jit(solution)/shard_map/dot_general | solution.py:147
  251.4 13.5 %multiply_convert_fusion = bf16[2048,1024]{1,0:T(8,128)(2,1)} fusion(f32[2048]{0:T(1024)S(1)} %bitcast.97, f32[2048,768]{1,0:T(8,128)} %fusion.5, bf16[2048,1024]{1,0:T(8,128)(2,1)} %bitcast.92, bf16[1,768,1024]{2,1,0:T(8,128)(2,1)} %param.15, bf16[1,1024,768]{2,1,0:T(8,128)(2,1)} %param.14), kind=kOutput, calls=%fused_computation | convolution fusion | flops 6456082432 | bytes 17833984 | tf_op jit(solution)/shard_map/dot_general | solution.py:150
  265.0 6.8 %convolution_convert_fusion = bf16[16,256,1024]{2,1,0:T(8,128)(2,1)} fusion(bf16[16,128,1024]{2,1,0:T(8,128)(2,1)} %bitcast.90, s32[16,256]{1,0:T(8,128)S(1)} %bitcast_select_fusion), kind=kOutput, calls=%fused_computation.1 | convolution fusion | flops 1078460416 | bytes 12599296 | tf_op jit(solution)/shard_map/sct,scl->stl/dot_general | solution.py:152
  271.8 105.0 %reduce-scatter.2.cloned.1.call-done.a_ref = bf16[256,1024]{1,0:T(8,128)(2,1)} async-done(((bf16[4096,1024]{1,0:T(8,128)(2,1)}), bf16[256,1024]{1,0:T(8,128)(2,1)}) %reduce-scatter.2.cloned.1.call-update) | async-done | bytes 524304 | tf_op jit(solution)/shard_map/reduce_scatter | solution.py:160
  376.9 3.4 copy-done.3
  380.2 1.6 copy-done.4
  381.8 1.0 copy-done.6
  382.9 5.9 %shard_map.83 = bf16[256,4096]{1,0:T(8,128)(2,1)} custom-call(bf16[256,1024]{1,0:T(8,128)(2,1)S(1)} %copy-done.6, bf16[8,512,1024]{2,1,0:T(8,128)(2,1)S(1)} %bitcast.84, bf16[256,4096]{1,0:T(8,128)(2,1)S(1)} %copy-done.4), custom_call_target="tpu_custom_call" | custom-call | tf_op jit(solution)/shard_map/pallas_call | solution.py:88
  (40 shorter events, 0.2 us)
Async XLA Ops:
  6.5 1.6 copy-start
  6.5 80.7 %all-gather.5.cloned.1.call-start = ((), (), s32[]{:S(2)}) async-start(), calls=%async_computation.2 | async-start | bytes 8912896 | tf_op jit(solution)/shard_map/all_gather | solution.py:14
  9.0 225.7 %all-gather.7.cloned.1.call-start = ((), (), s32[]{:S(2)}) async-start(), calls=%async_computation.3 | async-start | bytes 9469952 | tf_op jit(solution)/shard_map/all_gather | solution.py:124
  13.4 5.1 %copy-start.9 = (s32[256,4]{0,1:T(4,128)S(1)}, s32[256,4]{0,1:T(4,128)}, u32[]{:S(2)}) copy-start(s32[256,4]{0,1:T(4,128)} %param.9) | copy-start | bytes 12292
  13.4 5.1 %copy-start.10 = (s32[256,4]{0,1:T(4,128)S(1)}, s32[256,4]{0,1:T(4,128)}, u32[]{:S(2)}) copy-start(s32[256,4]{0,1:T(4,128)} %param.10) | copy-start | bytes 12292
  87.2 3.4 copy-start.5
  96.5 280.3 %reduce-scatter.2.cloned.1.call-start = ((), (), s32[]{:S(2)}) async-start(), calls=%async_computation.1 | async-start | bytes 8912896 | tf_op jit(solution)/shard_map/reduce_scatter | solution.py:160
  97.9 45.1 %collective-permute-start = (bf16[512,1024]{1,0:T(8,128)(2,1)S(1)}, bf16[512,1024]{1,0:T(8,128)(2,1)}, u32[]{:S(2)}, u32[]{:S(2)}) collective-permute-start(bf16[512,1024]{1,0:T(8,128)(2,1)S(1)} %constant_dynamic-slice_fusion), channel_id=1, source_target_pairs={{0,1},{1,2},{2,3},{3,0},{4,5},{5,6},{6,7},{7,4},{8,9},{9,10},{10,1... | collective-permute-start | bytes 3145736 | tf_op jit(solution)/shard_map/ppermute | solution.py:29
  143.0 49.2 %collective-permute-start.2 = (bf16[512,1024]{1,0:T(8,128)(2,1)}, bf16[512,1024]{1,0:T(8,128)(2,1)}, u32[]{:S(2)}, u32[]{:S(2)}) collective-permute-start(bf16[512,1024]{1,0:T(8,128)(2,1)} %collective-permute-done), channel_id=1, source_target_pairs={{0,1},{1,2},{2,3},{3,0},{4,5},{5,6},{6,7},{7,4},{8,9},{9,10},{10,1... | collective-permute-start | bytes 3145736 | tf_op jit(solution)/shard_map/ppermute | solution.py:29
  143.0 81.6 %collective-permute-start.4 = (bf16[512,1024]{1,0:T(8,128)(2,1)S(1)}, bf16[512,1024]{1,0:T(8,128)(2,1)}, u32[]{:S(2)}, u32[]{:S(2)}) collective-permute-start(bf16[512,1024]{1,0:T(8,128)(2,1)S(1)} %constant_dynamic-slice_fusion), channel_id=1, source_target_pairs={{0,3},{1,0},{2,1},{3,2},{4,7},{5,4},{6,5},{7,6},{8,11},{9,8},{10,9... | collective-permute-start | bytes 3145736 | tf_op jit(solution)/shard_map/ppermute | solution.py:29
  146.8 79.1 %collective-permute-start.1 = (bf16[512,1024]{1,0:T(8,128)(2,1)}, bf16[512,1024]{1,0:T(8,128)(2,1)}, u32[]{:S(2)}, u32[]{:S(2)}) collective-permute-start(bf16[512,1024]{1,0:T(8,128)(2,1)} %collective-permute-done), channel_id=1, source_target_pairs={{0,4},{4,0},{8,12},{12,8},{1,5},{5,1},{9,13},{13,9},{2,6},{6,2},{1... | collective-permute-start | bytes 3145736 | tf_op jit(solution)/shard_map/ppermute | solution.py:30
  192.2 36.4 %collective-permute-start.3 = (bf16[512,1024]{1,0:T(8,128)(2,1)}, bf16[512,1024]{1,0:T(8,128)(2,1)}, u32[]{:S(2)}, u32[]{:S(2)}) collective-permute-start(bf16[512,1024]{1,0:T(8,128)(2,1)} %collective-permute-done.2), channel_id=1, source_target_pairs={{0,4},{4,0},{8,12},{12,8},{1,5},{5,1},{9,13},{13,9},{2,6},{6,2},{1... | collective-permute-start | bytes 3145736 | tf_op jit(solution)/shard_map/ppermute | solution.py:30
  192.2 1.6 copy-start.8
  224.6 6.7 %collective-permute-start.5 = (bf16[512,1024]{1,0:T(8,128)(2,1)}, bf16[512,1024]{1,0:T(8,128)(2,1)S(1)}, u32[]{:S(2)}, u32[]{:S(2)}) collective-permute-start(bf16[512,1024]{1,0:T(8,128)(2,1)} %collective-permute-done.4), channel_id=1, source_target_pairs={{0,4},{4,0},{8,12},{12,8},{1,5},{5,1},{9,13},{13,9},{2,6},{6,2},{1... | collective-permute-start | bytes 3145736 | tf_op jit(solution)/shard_map/ppermute | solution.py:30
  231.4 3.3 copy-start.2
  237.2 8.9 %copy-start.11 = (bf16[1,1024,768]{2,1,0:T(8,128)(2,1)S(1)}, bf16[1,1024,768]{2,1,0:T(8,128)(2,1)}, u32[]{:S(2)}) copy-start(bf16[1,1024,768]{2,1,0:T(8,128)(2,1)} %param.13) | copy-start | bytes 4718596
  244.6 6.8 %copy-start.7 = (bf16[16,128,1024]{2,1,0:T(8,128)(2,1)}, bf16[16,128,1024]{2,1,0:T(8,128)(2,1)S(1)}, u32[]{:S(2)}) copy-start(bf16[16,128,1024]{2,1,0:T(8,128)(2,1)S(1)} %convolution_convert_fusion.1) | copy-start | bytes 12582916
  271.8 117.0 %copy-start.1 = (bf16[1024,1024]{1,0:T(8,128)(2,1)S(1)}, bf16[1024,1024]{1,0:T(8,128)(2,1)}, u32[]{:S(2)}) copy-start(bf16[1024,1024]{1,0:T(8,128)(2,1)} %param.11) | copy-start | bytes 6291460
  376.9 3.4 copy-start.3
  380.2 1.6 copy-start.4
  381.8 1.0 copy-start.6
Sparse Core Ops, SparseCore 0:
  9.6 77.5 all-gather.4
  96.7 127.4 all-gather.6
  271.9 104.8 reduce-scatter.1
